TPU v7x, 128 devices: a whole 4x4x4 slice. The times are simulated.
128 devices in a mesh: grp: 8 (over y, core), sp: 16 (over x, z).
Axes of the slice: x: 4, y: 4, z: 4, core: 2. Of those that a mesh axis runs over, the one named last changes fastest.
Arguments:
- frames: bfloat16 [16, 4, 32, 240, 384], P('grp', None, 'sp'), may hold values from -6 to 6
- conv_weight: bfloat16 [3, 3, 3, 384, 384], replicated, may hold values from -0.0625 to 0.0625
- conv_bias: float32 [384], replicated, may hold values from -4 to 4
- projection: bfloat16 [384, 16], replicated, may hold values from -0.3125 to 0.3125
Outputs:
- coded: bfloat16 [16, 16, 2, 240, 32], P('grp', None, None, 'sp')
All inputs are finite; a program needn't handle non-finite values.
Results may differ from a plain program's by a relative error of at most 0.0065.
Values may be sent and summed in bfloat16 or wider, within the bound.
No kernel may reach another device: no remote copies, remote signals or barrier semaphores. Data moves between devices by JAX's collectives and lax.ppermute only.
A program may use at most 192 MiB of HBM per device.

v0:
```python
import functools

import jax
import jax.numpy as jnp
from jax import lax
from jax.experimental import pallas as pl
from jax.experimental.pallas import tpu as pltpu
from jax.sharding import PartitionSpec as P

F32, BF16 = jnp.float32, jnp.bfloat16
HBM, VMEM = pltpu.MemorySpace.HBM, pltpu.MemorySpace.VMEM
IN_HBM, IN_VMEM = pl.BlockSpec(memory_space=HBM), pl.BlockSpec(memory_space=VMEM)
DMA = pltpu.SemaphoreType.DMA


def dot(a, b):
    return jnp.dot(a, b, preferred_element_type=F32)


def cost(macs, nbytes):
    return pl.CostEstimate(flops=2 * macs, bytes_accessed=nbytes, transcendentals=0)


def params(mib):
    return pltpu.CompilerParams(vmem_limit_bytes=mib * 2**20)


def spread_taps(x, taps, at):
    cols, chans = x.shape
    wide = x.astype(F32)
    col = lax.broadcasted_iota(jnp.int32, wide.shape, 0)
    before = jnp.where(col == 0, 0.0, pltpu.roll(wide, 1, 0)).astype(BF16)
    after = jnp.where(col == cols - 1, 0.0, pltpu.roll(wide, cols - 1, 0)).astype(BF16)
    base = at * 3 * chans
    taps[:, base : base + chans] = before
    taps[:, base + chans : base + 2 * chans] = x
    taps[:, base + 2 * chans : base + 3 * chans] = after


def in_hbm(*arrays):
    return [pltpu.with_memory_space_constraint(x, HBM) for x in arrays]


def in_vmem(x):
    return pltpu.with_memory_space_constraint(x, VMEM)


def odd_device():
    return lax.rem(lax.axis_index("sp"), 2)


def edge_terms(taps, w, o_ref):
    ch = w.shape[1]

    def term(f, low, high):
        return dot(
            taps[:, f * 3 * ch : (f + 1) * 3 * ch],
            w[:, :, low * ch : high * ch].reshape(3 * ch, (high - low) * ch),
        )

    both = term(1, 1, 3) + term(2, 0, 2)
    o_ref[0] = (both[:, :ch] + term(0, 2, 3)).astype(BF16)
    o_ref[1] = (both[:, ch:] + term(3, 0, 1)).astype(BF16)


def edge_sums(frames, weight, projection):
    clips, depth, rows, cols, ch = frames.shape
    latents = projection.shape[0]

    def kernel(
        x_hbm, w_hbm, p_hbm, near_ref, far_ref, near_taps, far_taps, inner, placed, x, w, p, x_sem, w_sem, i_sem, p_sem
    ):
        odd = odd_device()
        in_p = pltpu.make_async_copy(p_hbm, p, p_sem)
        in_x, in_w = [], []
        for e, (row, tap) in enumerate(((1 - odd, 2 * odd), (odd, 2 - 2 * odd))):
            in_x.append(
                [pltpu.make_async_copy(x_hbm.at[c, :, row], x.at[e, c], x_sem.at[e, c]) for c in range(clips)]
            )
            in_w.append(
                [
                    pltpu.make_async_copy(w_hbm.at[a, tap], w.at[e, :, :, pl.ds((2 - a) * ch, ch)], w_sem.at[e, a])
                    for a in range(3)
                ]
            )
        in_inner = [
            pltpu.make_async_copy(w_hbm.at[a, b], inner.at[a, :, :, pl.ds(place * ch, ch)], i_sem.at[a, place])
            for a in range(3)
            for place, b in enumerate((2 * odd, 1, 2 - 2 * odd))
        ]
        in_x[0][0].start()
        for copy in in_w[0]:
            copy.start()
        in_x[0][1].start()
        in_p.start()
        in_x[0][0].wait()
        for f in range(depth):
            spread_taps(x[0, 0, f], near_taps.at[0], f)
        in_p.wait()
        k = lax.broadcasted_iota(jnp.int32, (latents, 128), 0)
        lane = lax.broadcasted_iota(jnp.int32, (latents, 128), 1)
        for c in range(clips):
            for t in range(2):
                pick = (lane % 64 == t * 32 + c * latents + k).astype(F32).astype(BF16)
                turned = lax.dot_general(p[...], pick, (((0,), (0,)), ((), ())), preferred_element_type=F32)
                at = (c * 2 + t) * ch
                placed[at : at + ch] = turned.astype(BF16)
        for copy in in_w[0]:
            copy.wait()
        for copy in in_x[1] + in_w[1] + in_inner:
            copy.start()
        for e, (taps, o_ref) in enumerate(((near_taps, near_ref), (far_taps, far_ref))):
            for c in range(clips):
                if e + c > 0:
                    in_x[e][c].wait()
                    for f in range(depth):
                        spread_taps(x[e, c, f], taps.at[c], f)
                if e == 1 and c == 0:
                    for copy in in_w[e]:
                        copy.wait()
                edge_terms(taps.at[c], w.at[e], o_ref.at[c])
        for copy in in_inner:
            copy.wait()

    edge = jax.ShapeDtypeStruct((clips, 2, cols, ch), BF16)
    taps = pltpu.VMEM((clips, cols, depth * 3 * ch), BF16)
    return pl.pallas_call(
        kernel,
        in_specs=[IN_HBM] * 3,
        out_specs=[IN_VMEM] * 6,
        out_shape=[edge, edge, taps, taps, pltpu.VMEM((3, 3, ch, 3 * ch), BF16), pltpu.VMEM((4 * ch, 128), BF16)],
        scratch_shapes=[
            pltpu.VMEM((rows, clips, depth, cols, ch), BF16),
            pltpu.VMEM((rows, 3, ch, 3 * ch), BF16),
            pltpu.VMEM((latents, ch), BF16),
            DMA((rows, clips)),
            DMA((rows, 3)),
            DMA((3, 3)),
            DMA,
        ],
        compiler_params=params(20),
        cost_estimate=cost(clips * 4 * cols * 9 * ch * ch, 16 * 10**6),
    )(*in_hbm(frames, weight, projection))


def inner_sums(near, far, weight):
    clips, cols, _ = near.shape
    ch = weight.shape[2]

    def kernel(near, far, w, out):
        for c in range(clips):
            for t in range(2):
                window = slice(t * 3 * ch, (t + 3) * 3 * ch)
                out[c, t] = dot(near[c, :, window], w[:, :, :, ch:].reshape(9 * ch, 2 * ch)) + dot(
                    far[c, :, window], w[:, :, :, : 2 * ch].reshape(9 * ch, 2 * ch)
                )

    return pl.pallas_call(
        kernel,
        in_specs=[IN_VMEM] * 3,
        out_specs=IN_VMEM,
        out_shape=pltpu.VMEM((clips, 2, cols, 2 * ch), F32),
        compiler_params=params(16),
        cost_estimate=cost(clips * 8 * cols * 9 * ch * ch, 14 * 10**6),
    )(near, far, weight)


def latent_messages(sums, near, far, bias, placed, shards, groups):
    clips, outs, cols, wide = sums.shape
    ch = wide // 2
    lanes = placed.shape[1]
    half = lanes // 2
    share = cols // shards

    def over_channels(x, pick):
        x = pick(x, pltpu.roll(x, half // 4, 1))
        return pick(x, pltpu.roll(x, half // 2, 1))

    def in_terms(x):
        first = x.astype(BF16).astype(F32)
        second = (x - first).astype(BF16).astype(F32)
        third = x - first - second
        block = lax.broadcasted_iota(jnp.int32, x.shape, 1) // (half // 4)
        return jnp.where(block == 4, first, jnp.where(block == 5, second, jnp.where(block == 6, third, 0.0)))

    def kernel(s_ref, near_ref, far_ref, b_ref, p_ref, o_ref, hidden, latent):
        odd = odd_device()
        bias_row = b_ref[...]
        lowest = highest = None
        for part, (halo, row) in enumerate(((near_ref, 1 - odd), (far_ref, odd))):
            for c in range(clips):
                for t in range(outs):
                    v = s_ref[c, t, :, part * ch : (part + 1) * ch] + halo[c, t].astype(F32) + bias_row
                    v = v * 0.5
                    at = (c * outs + t) * ch
                    hidden[:, at : at + ch] = (v + v * jnp.tanh(v)).astype(BF16)
            found = dot(hidden[...], p_ref[...])
            latent[row, :cols] = found
            low = jnp.min(found, axis=0, keepdims=True)
            high = jnp.max(found, axis=0, keepdims=True)
            lowest = low if lowest is None else jnp.minimum(lowest, low)
            highest = high if highest is None else jnp.maximum(highest, high)
        latent[:, cols:] = jnp.zeros_like(latent[:, cols:])
        lowest = over_channels(lowest, jnp.minimum)
        highest = over_channels(highest, jnp.maximum)
        middle = (lowest + highest) * 0.5
        at_end = (lax.broadcasted_iota(jnp.int32, (8, lanes), 0) == 7) & (
            lax.broadcasted_iota(jnp.int32, (8, lanes), 1) >= half
        )
        in_front = lax.broadcasted_iota(jnp.int32, (8, lanes), 1) < half
        ends = (in_terms(lowest), in_terms(highest))
        for s in range(shards):
            rows = []
            for r in range(2):
                first = latent[r, pl.ds(share * s, 8)]
                second = latent[r, pl.ds(share * s + 8, 8)]
                rows.append(jnp.where(at_end, ends[r], jnp.where(in_front, first, second) - middle))
            message = jnp.concatenate(rows, axis=0).astype(BF16)
            for g in range(groups):
                o_ref[g, s] = message

    return pl.pallas_call(
        kernel,
        in_specs=[IN_VMEM] * 5,
        out_specs=IN_VMEM,
        out_shape=pltpu.VMEM((groups, shards, 16, lanes), BF16),
        scratch_shapes=[pltpu.VMEM((cols, clips * outs * ch), BF16), pltpu.VMEM((2, cols + 8, lanes), F32)],
        compiler_params=params(16),
        cost_estimate=cost(2 * cols * clips * outs * ch * lanes, 4 * 10**6),
    )(sums, near, far, bias, placed)


def coded_columns(received, share):
    groups, shards, _, lanes = received.shape
    latents = lanes // 8
    channels = lanes // 4

    def kernel(x_ref, o_ref, coded, turned):
        block = lax.broadcasted_iota(jnp.int32, (1, lanes), 1) // latents

        def end(g, row):
            terms = x_ref[g].astype(F32)[:, row, :]
            return terms + pltpu.roll(terms, lanes - latents, 1) + pltpu.roll(terms, lanes - 2 * latents, 1)

        def to_all(x):
            x = jnp.where(block == 4, x, 0.0)
            for step in (1, 2, 4):
                x = x + pltpu.roll(x, step * latents, 1)
            return x

        lows = [end(g, 7) for g in range(groups)]
        highs = [end(g, 15) for g in range(groups)]
        low = jnp.min(functools.reduce(jnp.minimum, lows), axis=0, keepdims=True)
        high = jnp.max(functools.reduce(jnp.maximum, highs), axis=0, keepdims=True)
        low, high = to_all(low), to_all(high)
        mine = lax.axis_index("grp")
        middle = to_all((end(mine, 7) + end(mine, 15)) * 0.5)
        x = x_ref[mine].astype(F32) + middle[:, None, :]
        coded[...] = ((x - low) / (high - low) * 2.0 - 1.0).reshape(shards * 16, lanes)
        for first in range(8):
            piece_of = coded[pl.ds(first, 2 * shards, stride=8), :].T
            for piece in range(4):
                w, t = first + 8 * (piece // 2), piece % 2
                if w < share:
                    rows = piece_of[piece * channels : (piece + 1) * channels]
                    turned[pl.ds(2 * w + t, channels, stride=2 * share), :] = rows
        o_ref[...] = turned[...].astype(BF16)

    return pl.pallas_call(
        kernel,
        in_specs=[IN_VMEM],
        out_specs=IN_VMEM,
        out_shape=jax.ShapeDtypeStruct((channels * share * 2, 2 * shards), BF16),
        scratch_shapes=[pltpu.VMEM((shards * 16, lanes), F32), pltpu.VMEM((channels * share * 2, 2 * shards), F32)],
        compiler_params=params(16),
    )(in_vmem(received))


def on_device(frames, conv_weight, conv_bias, projection):
    clips, depth, rows, cols, ch = frames.shape
    latents = projection.shape[1]
    outs = depth - 2
    shards, groups = lax.axis_size("sp"), lax.axis_size("grp")
    share = cols // shards

    def swap(x, first):
        pairs = [(i, i + 1) for i in range(first, shards - 1, 2)]
        return lax.ppermute(x, "sp", pairs + [(b, a) for a, b in pairs])

    near_sums, far_sums, near_taps, far_taps, inner_w, placed = edge_sums(frames, conv_weight, projection.T)
    near, far = swap(near_sums, 0), swap(far_sums, 1)
    sums = inner_sums(near_taps, far_taps, inner_w)

    messages = latent_messages(sums, near, far, conv_bias.reshape(1, ch), placed, shards, groups)
    messages = messages.reshape(groups * shards, 16, messages.shape[-1])
    received = lax.all_to_all(messages, ("grp", "sp"), 0, 0).reshape(groups, shards, 16, -1)
    coded = coded_columns(received, share)
    return coded.reshape(clips, latents, share, outs, rows * shards).transpose(0, 1, 3, 2, 4)


def solution(mesh):
    placed = (P("grp", None, "sp", None, None), P(), P(), P())
    return jax.shard_map(
        on_device,
        mesh=mesh,
        in_specs=placed,
        out_specs=P("grp", None, None, "sp", None),
        check_vma=False,
    )
```

profile of v0, /device:TPU:0, one launch (start us, length us, event | category | flops | bytes accessed | tf_op | source)
XLA Modules:
  0.0 59.9 jit_solution(10747042452973092433)
XLA Ops:
  0.0 0.0 copy-start
  0.0 10.1 %shard_map.46 = (bf16[2,2,240,384]{3,2,1,0:T(8,128)(2,1)S(1)}, bf16[2,2,240,384]{3,2,1,0:T(8,128)(2,1)S(1)}, bf16[2,240,4608]{2,1,0:T(8,128)(2,1)S(1)}, bf16[2,2...) custom-call(bf16[2,4,2,240,384]{4,3,2,1,0:T(8,128)(2,1)} %x_hbm.1, ...), custom_call_target="tpu_custom_call" | custom-call | flops 5096079360 | bytes 16000000 | tf_op jit(solution)/shard_map/pallas_call | solution.py:127
  10.2 2.0 %collective-permute-start = (bf16[2,2,240,384]{3,2,1,0:T(8,128)(2,1)S(1)}, bf16[2,2,240,384]{3,2,1,0:T(8,128)(2,1)S(1)}, u32[]{:S(2)}, u32[]{:S(2)}) collective-permute-start(bf16[2,2,240,384]{3,2,1,0:T(8,128)(2,1)S(1)} %get-tuple-element.14), channel_id=1, source_target_pairs={{0,1},{2,3},{4,5},{6,7},{8,9},{10,11},{12,13},{14,15},{1,0},{3,2},... | collective-permute-start | bytes 2211848 | tf_op jit(solution)/shard_map/ppermute | solution.py:288
  12.2 0.9 %collective-permute-start.1 = (bf16[2,2,240,384]{3,2,1,0:T(8,128)(2,1)S(1)}, bf16[2,2,240,384]{3,2,1,0:T(8,128)(2,1)S(1)}, u32[]{:S(2)}, u32[]{:S(2)}) collective-permute-start(bf16[2,2,240,384]{3,2,1,0:T(8,128)(2,1)S(1)} %get-tuple-element.15), channel_id=1, source_target_pairs={{1,2},{3,4},{5,6},{7,8},{9,10},{11,12},{13,14},{2,1},{4,3},{6,5},{... | collective-permute-start | bytes 2211848 | tf_op jit(solution)/shard_map/ppermute | solution.py:288
  13.1 0.0 copy-done
  13.1 10.8 %shard_map.47.s_ref = f32[2,2,240,768]{3,2,1,0:T(8,128)S(1)} custom-call(bf16[2,240,4608]{2,1,0:T(8,128)(2,1)S(1)} %get-tuple-element.11.near, bf16[2,240,4608]{2,1,0:T(8,128)(2,1)S(1)} %get-tuple-element.12.far, bf16[3,3,384,1152]{3,2,1,0:T(8,128)(2,1)S(1)} %get-tuple-element.13.w), custom_call_target="tpu_custom_call" | custom-call | flops 10192158720 | bytes 14000000 | tf_op jit(solution)/shard_map/pallas_call | solution.py:158
  23.9 4.8 %collective-permute-done.near_ref = bf16[2,2,240,384]{3,2,1,0:T(8,128)(2,1)S(1)} collective-permute-done((bf16[2,2,240,384]{3,2,1,0:T(8,128)(2,1)S(1)}, bf16[2,2,240,384]{3,2,1,0:T(8,128)(2,1)S(1)}, u32[]{:S(2)}, u32[]{:S(2)}) %collective-permute-start) | collective-permute-done | bytes 737312 | tf_op jit(solution)/shard_map/ppermute | solution.py:288
  28.7 0.0 collective-permute-done.1.far_ref
  28.7 1.4 %shard_map.48 = bf16[8,16,16,128]{3,2,1,0:T(8,128)(2,1)S(1)} custom-call(f32[2,2,240,768]{3,2,1,0:T(8,128)S(1)} %shard_map.47.s_ref, bf16[2,2,240,384]{3,2,1,0:T(8,128)(2,1)S(1)} %collective-permute-done.near_ref, bf16[2,2,240,384]{3,2,1,0:T(8,128)(2,1)S(1)} %collective-permute-done.1.far_ref, f32[1,384]{1,0:T(1,128)S(1)} %reshape.12.b_ref, ...), custom_call_target="tpu_custom_call" | custom-call | flops 188743680 | bytes 4000000 | tf_op jit(solution)/shard_map/pallas_call | solution.py:222
  30.1 28.5 %all_to_all.5 = bf16[128,16,128]{2,1,0:T(8,128)(2,1)S(1)} all-to-all(bf16[128,16,128]{2,1,0:T(8,128)(2,1)S(1)} %bitcast.6), channel_id=1, replica_groups=mesh['grp'=8,'sp'=16] {'grp','sp'}, dimensions={0} | all-to-all | bytes 1048576 | tf_op jit(solution)/shard_map/all_to_all | solution.py:296
  58.6 1.4 %shard_map.49 = bf16[960,32]{1,0:T(8,128)(2,1)} custom-call(bf16[8,16,16,128]{3,2,1,0:T(8,128)(2,1)S(1)} %bitcast.7), custom_call_target="tpu_custom_call" | custom-call | tf_op jit(solution)/shard_map/pallas_call | solution.py:269
  (1 shorter events, 0.0 us)
Async XLA Ops:
  0.0 13.1 %copy-start = (f32[384]{0:T(512)S(1)}, f32[384]{0:T(512)}, u32[]{:S(2)}) copy-start(f32[384]{0:T(512)} %param.6) | copy-start | bytes 4612
  10.2 18.5 %collective-permute-start = (bf16[2,2,240,384]{3,2,1,0:T(8,128)(2,1)S(1)}, bf16[2,2,240,384]{3,2,1,0:T(8,128)(2,1)S(1)}, u32[]{:S(2)}, u32[]{:S(2)}) collective-permute-start(bf16[2,2,240,384]{3,2,1,0:T(8,128)(2,1)S(1)} %get-tuple-element.14), channel_id=1, source_target_pairs={{0,1},{2,3},{4,5},{6,7},{8,9},{10,11},{12,13},{14,15},{1,0},{3,2},... | collective-permute-start | bytes 2211848 | tf_op jit(solution)/shard_map/ppermute | solution.py:288
  12.2 16.5 %collective-permute-start.1 = (bf16[2,2,240,384]{3,2,1,0:T(8,128)(2,1)S(1)}, bf16[2,2,240,384]{3,2,1,0:T(8,128)(2,1)S(1)}, u32[]{:S(2)}, u32[]{:S(2)}) collective-permute-start(bf16[2,2,240,384]{3,2,1,0:T(8,128)(2,1)S(1)} %get-tuple-element.15), channel_id=1, source_target_pairs={{1,2},{3,4},{5,6},{7,8},{9,10},{11,12},{13,14},{2,1},{4,3},{6,5},{... | collective-permute-start | bytes 2211848 | tf_op jit(solution)/shard_map/ppermute | solution.py:288
where the time goes:
time: 60.3 us; the launch traced here: 59.9 us
  blocking collectives  28.5 us (47%)
  Pallas kernels  23.7 us (39%)
  waiting for transfers between devices  4.79 us (8%)
  starting transfers between devices  2.9 us (5%)
    all_to_all x1, blocking collectives, on_device(): lax.all_to_all(messages, ('grp', 'sp'), 0, 0)  28.5 us
    pallas_call x1, Pallas kernels, inner_sums(): pl.pallas_call(kernel, in_specs=[IN_VMEM] * 3, out_specs=IN_VMEM, out_sha...  10.8 us
    pallas_call x1, Pallas kernels, edge_sums(): pl.pallas_call(kernel, in_specs=[IN_HBM] * 3, out_specs=[IN_VMEM] * 6, ou...  10.1 us
    ppermute x2, waiting for transfers between devices, swap(): return lax.ppermute(x, 'sp', pairs + [(b, a) for a, b in pairs])  4.79 us
    ppermute x2, starting transfers between devices, swap(): return lax.ppermute(x, 'sp', pairs + [(b, a) for a, b in pairs])  2.9 us
    pallas_call x1, Pallas kernels, latent_messages(): pl.pallas_call(kernel, in_specs=[IN_VMEM] * 5, out_specs=IN_VMEM, out_sha...  1.43 us
    pallas_call x1, Pallas kernels, coded_columns(): pl.pallas_call(kernel, in_specs=[IN_VMEM], out_specs=IN_VMEM, out_shape=j...  1.35 us
  transfers between devices with their start and end apart: 2, of which 1 were waited for; matrix products, arithmetic and copies ran while one was open for 0% of the time, Pallas kernels for 18%

commit v1 on v0

--- a/solution.py
+++ b/solution.py
@@ -50,17 +50,22 @@
 
 
 def edge_terms(taps, w, o_ref):
+    clips, cols, wide = taps.shape
     ch = w.shape[1]
 
     def term(f, low, high):
         return dot(
-            taps[:, f * 3 * ch : (f + 1) * 3 * ch],
+            taps[:, :, f * 3 * ch : (f + 1) * 3 * ch].reshape(clips * cols, 3 * ch),
             w[:, :, low * ch : high * ch].reshape(3 * ch, (high - low) * ch),
         )
 
     both = term(1, 1, 3) + term(2, 0, 2)
-    o_ref[0] = (both[:, :ch] + term(0, 2, 3)).astype(BF16)
-    o_ref[1] = (both[:, ch:] + term(3, 0, 1)).astype(BF16)
+    first = both[:, :ch] + term(0, 2, 3)
+    last = both[:, ch:] + term(3, 0, 1)
+    for c in range(clips):
+        rows = slice(c * cols, (c + 1) * cols)
+        o_ref[c, 0] = first[rows].astype(BF16)
+        o_ref[c, 1] = last[rows].astype(BF16)
 
 
 def edge_sums(frames, weight, projection):
@@ -107,18 +112,22 @@
                 placed[at : at + ch] = turned.astype(BF16)
         for copy in in_w[0]:
             copy.wait()
-        for copy in in_x[1] + in_w[1] + in_inner:
+        for copy in in_x[1] + in_w[1]:
             copy.start()
-        for e, (taps, o_ref) in enumerate(((near_taps, near_ref), (far_taps, far_ref))):
-            for c in range(clips):
-                if e + c > 0:
-                    in_x[e][c].wait()
-                    for f in range(depth):
-                        spread_taps(x[e, c, f], taps.at[c], f)
-                if e == 1 and c == 0:
-                    for copy in in_w[e]:
-                        copy.wait()
-                edge_terms(taps.at[c], w.at[e], o_ref.at[c])
+        edge_terms(near_taps.at[0:1], w.at[0], near_ref.at[0:1])
+        in_x[0][1].wait()
+        for f in range(depth):
+            spread_taps(x[0, 1, f], near_taps.at[1], f)
+        edge_terms(near_taps.at[1:2], w.at[0], near_ref.at[1:2])
+        for copy in in_inner:
+            copy.start()
+        for copy in in_w[1]:
+            copy.wait()
+        for c in range(clips):
+            in_x[1][c].wait()
+            for f in range(depth):
+                spread_taps(x[1, c, f], far_taps.at[c], f)
+            edge_terms(far_taps.at[c : c + 1], w.at[1], far_ref.at[c : c + 1])
         for copy in in_inner:
             copy.wait()
 
@@ -165,16 +174,50 @@
     )(near, far, weight)
 
 
-def latent_messages(sums, near, far, bias, placed, shards, groups):
+def row_latents(sums, part, halo, bias, placed, before=None):
     clips, outs, cols, wide = sums.shape
     ch = wide // 2
     lanes = placed.shape[1]
+
+    def over_channels(x, pick):
+        x = pick(x, pltpu.roll(x, lanes // 8, 1))
+        return pick(x, pltpu.roll(x, lanes // 4, 1))
+
+    def kernel(s_ref, halo_ref, b_ref, p_ref, *refs):
+        o_ref, ends_ref, hidden = refs[-3:]
+        for c in range(clips):
+            for t in range(outs):
+                v = s_ref[c, t, :, part * ch : (part + 1) * ch] + halo_ref[c, t].astype(F32) + b_ref[...]
+                v = v * 0.5
+                at = (c * outs + t) * ch
+                hidden[:, at : at + ch] = (v + v * jnp.tanh(v)).astype(BF16)
+        found = dot(hidden[...], p_ref[...])
+        o_ref[:cols] = found
+        o_ref[cols:] = jnp.zeros_like(o_ref[cols:])
+        low = over_channels(jnp.min(found, axis=0, keepdims=True), jnp.minimum)
+        high = over_channels(jnp.max(found, axis=0, keepdims=True), jnp.maximum)
+        first = lax.broadcasted_iota(jnp.int32, (8, lanes), 0) == 0
+        if before is None:
+            ends_ref[...] = jnp.where(first, low, high)
+        else:
+            ends_ref[...] = jnp.where(first, jnp.minimum(low, refs[0][...]), jnp.maximum(high, refs[0][...]))
+
+    args = [sums, halo, bias, placed] + ([] if before is None else [before])
+    return pl.pallas_call(
+        kernel,
+        in_specs=[IN_VMEM] * len(args),
+        out_specs=[IN_VMEM] * 2,
+        out_shape=[pltpu.VMEM((cols + 8, lanes), F32), pltpu.VMEM((8, lanes), F32)],
+        scratch_shapes=[pltpu.VMEM((cols, clips * outs * ch), BF16)],
+        compiler_params=params(16),
+        cost_estimate=cost(cols * clips * outs * ch * lanes, 2 * 10**6),
+    )(*args)
+
+
+def latent_messages(near, far, ends, other_ends, shards, copies):
+    padded, lanes = near.shape
     half = lanes // 2
-    share = cols // shards
-
-    def over_channels(x, pick):
-        x = pick(x, pltpu.roll(x, half // 4, 1))
-        return pick(x, pltpu.roll(x, half // 2, 1))
+    share = (padded - 8) // shards
 
     def in_terms(x):
         first = x.astype(BF16).astype(F32)
@@ -183,26 +226,12 @@
         block = lax.broadcasted_iota(jnp.int32, x.shape, 1) // (half // 4)
         return jnp.where(block == 4, first, jnp.where(block == 5, second, jnp.where(block == 6, third, 0.0)))
 
-    def kernel(s_ref, near_ref, far_ref, b_ref, p_ref, o_ref, hidden, latent):
+    def kernel(near_ref, far_ref, e_ref, other_ref, o_ref, latent):
         odd = odd_device()
-        bias_row = b_ref[...]
-        lowest = highest = None
-        for part, (halo, row) in enumerate(((near_ref, 1 - odd), (far_ref, odd))):
-            for c in range(clips):
-                for t in range(outs):
-                    v = s_ref[c, t, :, part * ch : (part + 1) * ch] + halo[c, t].astype(F32) + bias_row
-                    v = v * 0.5
-                    at = (c * outs + t) * ch
-                    hidden[:, at : at + ch] = (v + v * jnp.tanh(v)).astype(BF16)
-            found = dot(hidden[...], p_ref[...])
-            latent[row, :cols] = found
-            low = jnp.min(found, axis=0, keepdims=True)
-            high = jnp.max(found, axis=0, keepdims=True)
-            lowest = low if lowest is None else jnp.minimum(lowest, low)
-            highest = high if highest is None else jnp.maximum(highest, high)
-        latent[:, cols:] = jnp.zeros_like(latent[:, cols:])
-        lowest = over_channels(lowest, jnp.minimum)
-        highest = over_channels(highest, jnp.maximum)
+        latent[1 - odd] = near_ref[...]
+        latent[odd] = far_ref[...]
+        lowest = jnp.minimum(e_ref[0:1], other_ref[0:1])
+        highest = jnp.maximum(e_ref[1:2], other_ref[1:2])
         middle = (lowest + highest) * 0.5
         at_end = (lax.broadcasted_iota(jnp.int32, (8, lanes), 0) == 7) & (
             lax.broadcasted_iota(jnp.int32, (8, lanes), 1) >= half
@@ -216,18 +245,17 @@
                 second = latent[r, pl.ds(share * s + 8, 8)]
                 rows.append(jnp.where(at_end, ends[r], jnp.where(in_front, first, second) - middle))
             message = jnp.concatenate(rows, axis=0).astype(BF16)
-            for g in range(groups):
+            for g in range(copies):
                 o_ref[g, s] = message
 
     return pl.pallas_call(
         kernel,
-        in_specs=[IN_VMEM] * 5,
+        in_specs=[IN_VMEM] * 4,
         out_specs=IN_VMEM,
-        out_shape=pltpu.VMEM((groups, shards, 16, lanes), BF16),
-        scratch_shapes=[pltpu.VMEM((cols, clips * outs * ch), BF16), pltpu.VMEM((2, cols + 8, lanes), F32)],
+        out_shape=pltpu.VMEM((copies, shards, 16, lanes), BF16),
+        scratch_shapes=[pltpu.VMEM((2, padded, lanes), F32)],
         compiler_params=params(16),
-        cost_estimate=cost(2 * cols * clips * outs * ch * lanes, 4 * 10**6),
-    )(sums, near, far, bias, placed)
+    )(near, far, ends, other_ends)
 
 
 def coded_columns(received, share):
@@ -253,7 +281,7 @@
         low = jnp.min(functools.reduce(jnp.minimum, lows), axis=0, keepdims=True)
         high = jnp.max(functools.reduce(jnp.maximum, highs), axis=0, keepdims=True)
         low, high = to_all(low), to_all(high)
-        mine = lax.axis_index("grp")
+        mine = lax.div(lax.axis_index("grp"), 2)
         middle = to_all((end(mine, 7) + end(mine, 15)) * 0.5)
         x = x_ref[mine].astype(F32) + middle[:, None, :]
         coded[...] = ((x - low) / (high - low) * 2.0 - 1.0).reshape(shards * 16, lanes)
@@ -291,10 +319,15 @@
     near, far = swap(near_sums, 0), swap(far_sums, 1)
     sums = inner_sums(near_taps, far_taps, inner_w)
 
-    messages = latent_messages(sums, near, far, conv_bias.reshape(1, ch), placed, shards, groups)
-    messages = messages.reshape(groups * shards, 16, messages.shape[-1])
-    received = lax.all_to_all(messages, ("grp", "sp"), 0, 0).reshape(groups, shards, 16, -1)
-    coded = coded_columns(received, share)
+    bias = conv_bias.reshape(1, ch)
+    near_latents, near_ends = row_latents(sums, 0, near, bias, placed)
+    far_latents, ends = row_latents(sums, 1, far, bias, placed, near_ends)
+    other_ends = lax.ppermute(ends, "grp", [(i, i ^ 1) for i in range(groups)])
+    messages = latent_messages(near_latents, far_latents, ends, other_ends, shards, groups // 2)
+    messages = messages.reshape(groups // 2 * shards, 16, messages.shape[-1])
+    same_core = [[(2 * y + core) * shards + s for y in range(groups // 2) for s in range(shards)] for core in range(2)]
+    received = lax.all_to_all(messages, ("grp", "sp"), 0, 0, axis_index_groups=same_core)
+    coded = coded_columns(received.reshape(groups // 2, shards, 16, -1), share)
     return coded.reshape(clips, latents, share, outs, rows * shards).transpose(0, 1, 3, 2, 4)
 
 

time: 60.3 us -> 57.7 us (0.957)
  blocking collectives: 28.5 us -> 25.3 us
  waiting for transfers between devices: 4.79 us -> 5.97 us
    all_to_all x1, blocking collectives: 28.5 us -> 25.3 us  [on_device(): lax.all_to_all(messages, ('grp', 'sp'), 0, 0, axis_index_groups=same_core)]
    ppermute x0 -> x1, waiting for transfers between devices: none -> 1.17 us  [on_device(): other_ends = lax.ppermute(ends, 'grp', [(i, i ^ 1) for i in range(groups)])]
    pallas_call x1 -> x3, Pallas kernels: 1.43 us -> 1.65 us  [the longest x2 1.59 us: row_latents(): pl.pallas_call(kernel, in_specs=[IN_VMEM] * len(args), out_specs=[IN_VMEM...]
  transfers between devices with their start and end apart: 2 -> 3, of which waited for: 1 -> 2; matrix products, arithmetic and copies ran while one was open for 0% -> 0% of each run, Pallas kernels for 18% -> 20%
where the time goes in v1:
time: 57.7 us; the launch traced here: 57.5 us
  blocking collectives  25.3 us (44%)
  Pallas kernels  23.3 us (40%)
  waiting for transfers between devices  5.97 us (10%)
  starting transfers between devices  2.89 us (5%)
    all_to_all x1, blocking collectives, on_device(): lax.all_to_all(messages, ('grp', 'sp'), 0, 0, axis_index_groups=same_core)  25.3 us
    pallas_call x1, Pallas kernels, inner_sums(): pl.pallas_call(kernel, in_specs=[IN_VMEM] * 3, out_specs=IN_VMEM, out_sha...  10.8 us
    pallas_call x1, Pallas kernels, edge_sums(): pl.pallas_call(kernel, in_specs=[IN_HBM] * 3, out_specs=[IN_VMEM] * 6, ou...  9.58 us
    ppermute x2, waiting for transfers between devices, swap(): return lax.ppermute(x, 'sp', pairs + [(b, a) for a, b in pairs])  4.79 us
    ppermute x2, starting transfers between devices, swap(): return lax.ppermute(x, 'sp', pairs + [(b, a) for a, b in pairs])  2.89 us
    pallas_call x2, Pallas kernels, row_latents(): pl.pallas_call(kernel, in_specs=[IN_VMEM] * len(args), out_specs=[IN_VMEM...  1.59 us
    pallas_call x1, Pallas kernels, coded_columns(): pl.pallas_call(kernel, in_specs=[IN_VMEM], out_specs=IN_VMEM, out_shape=j...  1.31 us
    ppermute x1, waiting for transfers between devices, on_device(): other_ends = lax.ppermute(ends, 'grp', [(i, i ^ 1) for i in range(groups)])  1.17 us
  transfers between devices with their start and end apart: 3, of which 2 were waited for; matrix products, arithmetic and copies ran while one was open for 0% of the time, Pallas kernels for 20%

profile of v1, /device:TPU:0, one launch (start us, length us, event | category | flops | bytes accessed | tf_op | source)
XLA Modules:
  0.0 57.5 jit_solution(17322657192149761857)
XLA Ops:
  0.0 0.0 copy-start
  0.0 9.6 %shard_map.46 = (bf16[2,2,240,384]{3,2,1,0:T(8,128)(2,1)S(1)}, bf16[2,2,240,384]{3,2,1,0:T(8,128)(2,1)S(1)}, bf16[2,240,4608]{2,1,0:T(8,128)(2,1)S(1)}, bf16[2,2...) custom-call(bf16[2,4,2,240,384]{4,3,2,1,0:T(8,128)(2,1)} %x_hbm.1, ...), custom_call_target="tpu_custom_call" | custom-call | flops 5096079360 | bytes 16000000 | tf_op jit(solution)/shard_map/pallas_call | solution.py:136
  9.6 2.0 %collective-permute-start = (bf16[2,2,240,384]{3,2,1,0:T(8,128)(2,1)S(1)}, bf16[2,2,240,384]{3,2,1,0:T(8,128)(2,1)S(1)}, u32[]{:S(2)}, u32[]{:S(2)}) collective-permute-start(bf16[2,2,240,384]{3,2,1,0:T(8,128)(2,1)S(1)} %get-tuple-element.18), channel_id=1, source_target_pairs={{0,1},{2,3},{4,5},{6,7},{8,9},{10,11},{12,13},{14,15},{1,0},{3,2},... | collective-permute-start | bytes 2211848 | tf_op jit(solution)/shard_map/ppermute | solution.py:316
  11.6 0.9 %collective-permute-start.1 = (bf16[2,2,240,384]{3,2,1,0:T(8,128)(2,1)S(1)}, bf16[2,2,240,384]{3,2,1,0:T(8,128)(2,1)S(1)}, u32[]{:S(2)}, u32[]{:S(2)}) collective-permute-start(bf16[2,2,240,384]{3,2,1,0:T(8,128)(2,1)S(1)} %get-tuple-element.21), channel_id=1, source_target_pairs={{1,2},{3,4},{5,6},{7,8},{9,10},{11,12},{13,14},{2,1},{4,3},{6,5},{... | collective-permute-start | bytes 2211848 | tf_op jit(solution)/shard_map/ppermute | solution.py:316
  12.5 0.0 copy-done
  12.5 10.8 %shard_map.47.s_ref = f32[2,2,240,768]{3,2,1,0:T(8,128)S(1)} custom-call(bf16[2,240,4608]{2,1,0:T(8,128)(2,1)S(1)} %get-tuple-element.15.near, bf16[2,240,4608]{2,1,0:T(8,128)(2,1)S(1)} %get-tuple-element.16.far, bf16[3,3,384,1152]{3,2,1,0:T(8,128)(2,1)S(1)} %get-tuple-element.17.w), custom_call_target="tpu_custom_call" | custom-call | flops 10192158720 | bytes 14000000 | tf_op jit(solution)/shard_map/pallas_call | solution.py:167
  23.3 4.8 %collective-permute-done.halo_ref = bf16[2,2,240,384]{3,2,1,0:T(8,128)(2,1)S(1)} collective-permute-done((bf16[2,2,240,384]{3,2,1,0:T(8,128)(2,1)S(1)}, bf16[2,2,240,384]{3,2,1,0:T(8,128)(2,1)S(1)}, u32[]{:S(2)}, u32[]{:S(2)}) %collective-permute-start) | collective-permute-done | bytes 737312 | tf_op jit(solution)/shard_map/ppermute | solution.py:316
  28.1 0.8 %shard_map.48 = (f32[248,128]{1,0:T(8,128)S(1)}, f32[8,128]{1,0:T(8,128)S(1)}) custom-call(f32[2,2,240,768]{3,2,1,0:T(8,128)S(1)} %shard_map.47.s_ref, bf16[2,2,240,384]{3,2,1,0:T(8,128)(2,1)S(1)} %collective-permute-done.halo_ref, f32[1,384]{1,0:T(1,128)S(1)} %reshape.12.b_ref, bf16[1536,128]{1,0:T(8,128)(2,1)S(1)} %get-tuple-element.19.p_ref), custom_call_target="tpu_custom_call" | custom-call | flops 94371840 | bytes 2000000 | tf_op jit(solution)/shard_map/pallas_call | solution.py:206
  28.9 0.0 collective-permute-done.1.halo_ref
  28.9 0.8 %shard_map.49 = (f32[248,128]{1,0:T(8,128)S(1)}, f32[8,128]{1,0:T(8,128)S(1)}) custom-call(f32[2,2,240,768]{3,2,1,0:T(8,128)S(1)} %shard_map.47.s_ref, bf16[2,2,240,384]{3,2,1,0:T(8,128)(2,1)S(1)} %collective-permute-done.1.halo_ref, f32[1,384]{1,0:T(1,128)S(1)} %reshape.12.b_ref, bf16[1536,128]{1,0:T(8,128)(2,1)S(1)} %get-tuple-element.19.p_ref, ...), custom_call_target="tpu_custom_call" | custom-call | flops 94371840 | bytes 2000000 | tf_op jit(solution)/shard_map/pallas_call | solution.py:206
  29.7 0.0 collective-permute-start.2
  29.7 1.2 %collective-permute-done.2.other_ref = f32[8,128]{1,0:T(8,128)S(1)} collective-permute-done((f32[8,128]{1,0:T(8,128)S(1)}, f32[8,128]{1,0:T(8,128)S(1)}, u32[]{:S(2)}, u32[]{:S(2)}) %collective-permute-start.2) | collective-permute-done | bytes 4128 | tf_op jit(solution)/shard_map/ppermute | solution.py:325
  30.9 0.1 shard_map.50
  30.9 25.3 %all_to_all.5 = bf16[64,16,128]{2,1,0:T(8,128)(2,1)S(1)} all-to-all(bf16[64,16,128]{2,1,0:T(8,128)(2,1)S(1)} %bitcast.6), channel_id=1, replica_groups={{0,1,2,3,4,5,6,7,8,9,10,11,12,13,14,15,32,33,34,35,36,37,38,39,40,41,42..., dimensions={0} | all-to-all | bytes 524288 | tf_op jit(solution)/shard_map/all_to_all | solution.py:329
  56.2 1.3 %shard_map.51 = bf16[960,32]{1,0:T(8,128)(2,1)} custom-call(bf16[4,16,16,128]{3,2,1,0:T(8,128)(2,1)S(1)} %bitcast.7), custom_call_target="tpu_custom_call" | custom-call | tf_op jit(solution)/shard_map/pallas_call | solution.py:297
  (1 shorter events, 0.0 us)
Async XLA Ops:
  0.0 12.5 %copy-start = (f32[384]{0:T(512)S(1)}, f32[384]{0:T(512)}, u32[]{:S(2)}) copy-start(f32[384]{0:T(512)} %param.6) | copy-start | bytes 4612
  9.6 18.5 %collective-permute-start = (bf16[2,2,240,384]{3,2,1,0:T(8,128)(2,1)S(1)}, bf16[2,2,240,384]{3,2,1,0:T(8,128)(2,1)S(1)}, u32[]{:S(2)}, u32[]{:S(2)}) collective-permute-start(bf16[2,2,240,384]{3,2,1,0:T(8,128)(2,1)S(1)} %get-tuple-element.18), channel_id=1, source_target_pairs={{0,1},{2,3},{4,5},{6,7},{8,9},{10,11},{12,13},{14,15},{1,0},{3,2},... | collective-permute-start | bytes 2211848 | tf_op jit(solution)/shard_map/ppermute | solution.py:316
  11.6 17.3 %collective-permute-start.1 = (bf16[2,2,240,384]{3,2,1,0:T(8,128)(2,1)S(1)}, bf16[2,2,240,384]{3,2,1,0:T(8,128)(2,1)S(1)}, u32[]{:S(2)}, u32[]{:S(2)}) collective-permute-start(bf16[2,2,240,384]{3,2,1,0:T(8,128)(2,1)S(1)} %get-tuple-element.21), channel_id=1, source_target_pairs={{1,2},{3,4},{5,6},{7,8},{9,10},{11,12},{13,14},{2,1},{4,3},{6,5},{... | collective-permute-start | bytes 2211848 | tf_op jit(solution)/shard_map/ppermute | solution.py:316
  29.7 1.2 %collective-permute-start.2 = (f32[8,128]{1,0:T(8,128)S(1)}, f32[8,128]{1,0:T(8,128)S(1)}, u32[]{:S(2)}, u32[]{:S(2)}) collective-permute-start(f32[8,128]{1,0:T(8,128)S(1)} %get-tuple-element.24.e_ref), channel_id=1, source_target_pairs={{0,16},{16,0},{32,48},{48,32},{64,80},{80,64},{96,112},{112,96},{1... | collective-permute-start | bytes 12296 | tf_op jit(solution)/shard_map/ppermute | solution.py:325

commit v2 on v1

--- a/solution.py
+++ b/solution.py
@@ -50,57 +50,52 @@
 
 
 def edge_terms(taps, w, o_ref):
-    clips, cols, wide = taps.shape
     ch = w.shape[1]
 
     def term(f, low, high):
         return dot(
-            taps[:, :, f * 3 * ch : (f + 1) * 3 * ch].reshape(clips * cols, 3 * ch),
+            taps[:, f * 3 * ch : (f + 1) * 3 * ch],
             w[:, :, low * ch : high * ch].reshape(3 * ch, (high - low) * ch),
         )
 
     both = term(1, 1, 3) + term(2, 0, 2)
-    first = both[:, :ch] + term(0, 2, 3)
-    last = both[:, ch:] + term(3, 0, 1)
-    for c in range(clips):
-        rows = slice(c * cols, (c + 1) * cols)
-        o_ref[c, 0] = first[rows].astype(BF16)
-        o_ref[c, 1] = last[rows].astype(BF16)
-
-
-def edge_sums(frames, weight, projection):
-    clips, depth, rows, cols, ch = frames.shape
+    o_ref[0] = (both[:, :ch] + term(0, 2, 3)).astype(BF16)
+    o_ref[1] = (both[:, ch:] + term(3, 0, 1)).astype(BF16)
+
+
+def first_edges(frames, weight, projection):
+    clips, depth, _, cols, ch = frames.shape
     latents = projection.shape[0]
 
     def kernel(
-        x_hbm, w_hbm, p_hbm, near_ref, far_ref, near_taps, far_taps, inner, placed, x, w, p, x_sem, w_sem, i_sem, p_sem
+        x_hbm, w_hbm, p_hbm, near_ref, far_ref, near_taps, far_taps, x1, far_w, inner, placed,
+        x, w, p, x_sem, w_sem, i_sem, p_sem,
     ):
         odd = odd_device()
         in_p = pltpu.make_async_copy(p_hbm, p, p_sem)
-        in_x, in_w = [], []
-        for e, (row, tap) in enumerate(((1 - odd, 2 * odd), (odd, 2 - 2 * odd))):
-            in_x.append(
-                [pltpu.make_async_copy(x_hbm.at[c, :, row], x.at[e, c], x_sem.at[e, c]) for c in range(clips)]
-            )
-            in_w.append(
-                [
-                    pltpu.make_async_copy(w_hbm.at[a, tap], w.at[e, :, :, pl.ds((2 - a) * ch, ch)], w_sem.at[e, a])
-                    for a in range(3)
-                ]
-            )
+        in_near = [pltpu.make_async_copy(x_hbm.at[c, :, 1 - odd], x.at[c], x_sem.at[c]) for c in range(clips)]
+        in_far = pltpu.make_async_copy(x_hbm.at[0, :, odd], x.at[2], x_sem.at[2])
+        in_far1 = pltpu.make_async_copy(x_hbm.at[1, :, odd], x1, x_sem.at[3])
+        in_w, in_far_w = (
+            [
+                pltpu.make_async_copy(w_hbm.at[a, tap], to.at[:, :, pl.ds((2 - a) * ch, ch)], w_sem.at[e, a])
+                for a in range(3)
+            ]
+            for e, (tap, to) in enumerate(((2 * odd, w), (2 - 2 * odd, far_w)))
+        )
         in_inner = [
             pltpu.make_async_copy(w_hbm.at[a, b], inner.at[a, :, :, pl.ds(place * ch, ch)], i_sem.at[a, place])
             for a in range(3)
             for place, b in enumerate((2 * odd, 1, 2 - 2 * odd))
         ]
-        in_x[0][0].start()
-        for copy in in_w[0]:
+        in_near[0].start()
+        for copy in in_w:
             copy.start()
-        in_x[0][1].start()
+        in_near[1].start()
         in_p.start()
-        in_x[0][0].wait()
+        in_near[0].wait()
         for f in range(depth):
-            spread_taps(x[0, 0, f], near_taps.at[0], f)
+            spread_taps(x[0, f], near_taps.at[0], f)
         in_p.wait()
         k = lax.broadcasted_iota(jnp.int32, (latents, 128), 0)
         lane = lax.broadcasted_iota(jnp.int32, (latents, 128), 1)
@@ -110,108 +105,155 @@
                 turned = lax.dot_general(p[...], pick, (((0,), (0,)), ((), ())), preferred_element_type=F32)
                 at = (c * 2 + t) * ch
                 placed[at : at + ch] = turned.astype(BF16)
-        for copy in in_w[0]:
+        for copy in in_w:
             copy.wait()
-        for copy in in_x[1] + in_w[1]:
+        for copy in [in_far, *in_far_w, in_far1]:
             copy.start()
-        edge_terms(near_taps.at[0:1], w.at[0], near_ref.at[0:1])
-        in_x[0][1].wait()
+        edge_terms(near_taps.at[0], w, near_ref.at[0])
+        in_near[1].wait()
         for f in range(depth):
-            spread_taps(x[0, 1, f], near_taps.at[1], f)
-        edge_terms(near_taps.at[1:2], w.at[0], near_ref.at[1:2])
+            spread_taps(x[1, f], near_taps.at[1], f)
         for copy in in_inner:
             copy.start()
-        for copy in in_w[1]:
+        edge_terms(near_taps.at[1], w, near_ref.at[1])
+        in_far.wait()
+        for f in range(depth):
+            spread_taps(x[2, f], far_taps, f)
+        for copy in in_far_w:
             copy.wait()
-        for c in range(clips):
-            in_x[1][c].wait()
-            for f in range(depth):
-                spread_taps(x[1, c, f], far_taps.at[c], f)
-            edge_terms(far_taps.at[c : c + 1], w.at[1], far_ref.at[c : c + 1])
-        for copy in in_inner:
+        edge_terms(far_taps, far_w, far_ref)
+        for copy in [in_far1, *in_inner]:
             copy.wait()
 
-    edge = jax.ShapeDtypeStruct((clips, 2, cols, ch), BF16)
-    taps = pltpu.VMEM((clips, cols, depth * 3 * ch), BF16)
     return pl.pallas_call(
         kernel,
         in_specs=[IN_HBM] * 3,
-        out_specs=[IN_VMEM] * 6,
-        out_shape=[edge, edge, taps, taps, pltpu.VMEM((3, 3, ch, 3 * ch), BF16), pltpu.VMEM((4 * ch, 128), BF16)],
+        out_specs=[IN_VMEM] * 8,
+        out_shape=[
+            pltpu.VMEM((clips, 2, cols, ch), BF16),
+            pltpu.VMEM((2, cols, ch), BF16),
+            pltpu.VMEM((clips, cols, depth * 3 * ch), BF16),
+            pltpu.VMEM((cols, depth * 3 * ch), BF16),
+            pltpu.VMEM((depth, cols, ch), BF16),
+            pltpu.VMEM((3, ch, 3 * ch), BF16),
+            pltpu.VMEM((3, 3, ch, 3 * ch), BF16),
+            pltpu.VMEM((clips * 2 * ch, 128), BF16),
+        ],
         scratch_shapes=[
-            pltpu.VMEM((rows, clips, depth, cols, ch), BF16),
-            pltpu.VMEM((rows, 3, ch, 3 * ch), BF16),
+            pltpu.VMEM((3, depth, cols, ch), BF16),
+            pltpu.VMEM((3, ch, 3 * ch), BF16),
             pltpu.VMEM((latents, ch), BF16),
-            DMA((rows, clips)),
-            DMA((rows, 3)),
+            DMA((4,)),
+            DMA((2, 3)),
             DMA((3, 3)),
             DMA,
         ],
-        compiler_params=params(20),
-        cost_estimate=cost(clips * 4 * cols * 9 * ch * ch, 16 * 10**6),
+        compiler_params=params(16),
     )(*in_hbm(frames, weight, projection))
+
+
+def last_edges(x1, edge_w):
+    depth, cols, ch = x1.shape
+
+    def kernel(x, w, o_ref, taps):
+        for f in range(depth):
+            spread_taps(x[f], taps, f)
+        edge_terms(taps, w, o_ref)
+
+    return pl.pallas_call(
+        kernel,
+        in_specs=[IN_VMEM] * 2,
+        out_specs=[IN_VMEM] * 2,
+        out_shape=[pltpu.VMEM((2, cols, ch), BF16), pltpu.VMEM((cols, depth * 3 * ch), BF16)],
+        compiler_params=params(16),
+    )(x1, edge_w)
 
 
 def inner_sums(near, far, weight):
     clips, cols, _ = near.shape
     ch = weight.shape[2]
 
-    def kernel(near, far, w, out):
-        for c in range(clips):
+    def kernel(near, far0, far1, w, out):
+        for c, far in enumerate((far0, far1)):
             for t in range(2):
                 window = slice(t * 3 * ch, (t + 3) * 3 * ch)
                 out[c, t] = dot(near[c, :, window], w[:, :, :, ch:].reshape(9 * ch, 2 * ch)) + dot(
-                    far[c, :, window], w[:, :, :, : 2 * ch].reshape(9 * ch, 2 * ch)
+                    far[:, window], w[:, :, :, : 2 * ch].reshape(9 * ch, 2 * ch)
                 )
 
     return pl.pallas_call(
         kernel,
-        in_specs=[IN_VMEM] * 3,
+        in_specs=[IN_VMEM] * 4,
         out_specs=IN_VMEM,
         out_shape=pltpu.VMEM((clips, 2, cols, 2 * ch), F32),
         compiler_params=params(16),
-        cost_estimate=cost(clips * 8 * cols * 9 * ch * ch, 14 * 10**6),
-    )(near, far, weight)
-
-
-def row_latents(sums, part, halo, bias, placed, before=None):
+    )(near, *far, weight)
+
+
+def over_channels(x, pick):
+    lanes = x.shape[1]
+    x = pick(x, pltpu.roll(x, lanes // 8, 1))
+    return pick(x, pltpu.roll(x, lanes // 4, 1))
+
+
+def hidden_units(sums, halo, bias):
+    h = (sums + halo.astype(F32) + bias) * 0.5
+    return (h + h * jnp.tanh(h)).astype(BF16)
+
+
+def first_latents(sums, near, far0, bias, placed):
     clips, outs, cols, wide = sums.shape
     ch = wide // 2
     lanes = placed.shape[1]
 
-    def over_channels(x, pick):
-        x = pick(x, pltpu.roll(x, lanes // 8, 1))
-        return pick(x, pltpu.roll(x, lanes // 4, 1))
-
-    def kernel(s_ref, halo_ref, b_ref, p_ref, *refs):
-        o_ref, ends_ref, hidden = refs[-3:]
+    def kernel(s_ref, near_ref, far0_ref, b_ref, p_ref, near_out, far_out, ends_ref, hidden):
         for c in range(clips):
             for t in range(outs):
-                v = s_ref[c, t, :, part * ch : (part + 1) * ch] + halo_ref[c, t].astype(F32) + b_ref[...]
-                v = v * 0.5
                 at = (c * outs + t) * ch
-                hidden[:, at : at + ch] = (v + v * jnp.tanh(v)).astype(BF16)
-        found = dot(hidden[...], p_ref[...])
-        o_ref[:cols] = found
-        o_ref[cols:] = jnp.zeros_like(o_ref[cols:])
+                hidden[0, :, at : at + ch] = hidden_units(s_ref[c, t, :, :ch], near_ref[c, t], b_ref[...])
+        for t in range(outs):
+            hidden[1, :, t * ch : (t + 1) * ch] = hidden_units(s_ref[0, t, :, ch:], far0_ref[t], b_ref[...])
+        found = dot(hidden[0], p_ref[...])
+        near_out[:cols] = found
+        near_out[cols:] = jnp.zeros_like(near_out[cols:])
+        far_out[...] = dot(hidden[1, :, : outs * ch], p_ref[: outs * ch])
         low = over_channels(jnp.min(found, axis=0, keepdims=True), jnp.minimum)
         high = over_channels(jnp.max(found, axis=0, keepdims=True), jnp.maximum)
-        first = lax.broadcasted_iota(jnp.int32, (8, lanes), 0) == 0
-        if before is None:
-            ends_ref[...] = jnp.where(first, low, high)
-        else:
-            ends_ref[...] = jnp.where(first, jnp.minimum(low, refs[0][...]), jnp.maximum(high, refs[0][...]))
-
-    args = [sums, halo, bias, placed] + ([] if before is None else [before])
-    return pl.pallas_call(
-        kernel,
-        in_specs=[IN_VMEM] * len(args),
+        ends_ref[...] = jnp.where(lax.broadcasted_iota(jnp.int32, (8, lanes), 0) == 0, low, high)
+
+    return pl.pallas_call(
+        kernel,
+        in_specs=[IN_VMEM] * 5,
+        out_specs=[IN_VMEM] * 3,
+        out_shape=[pltpu.VMEM((cols + 8, lanes), F32), pltpu.VMEM((cols, lanes), F32), pltpu.VMEM((8, lanes), F32)],
+        scratch_shapes=[pltpu.VMEM((2, cols, clips * outs * ch), BF16)],
+        compiler_params=params(16),
+    )(sums, near, far0, bias, placed)
+
+
+def last_latents(sums, far1, bias, placed, far_latents0, near_ends):
+    clips, outs, cols, wide = sums.shape
+    ch = wide // 2
+    lanes = placed.shape[1]
+
+    def kernel(s_ref, far1_ref, b_ref, p_ref, far0_ref, near_ref, far_out, ends_ref, hidden):
+        for t in range(outs):
+            hidden[:, t * ch : (t + 1) * ch] = hidden_units(s_ref[1, t, :, ch:], far1_ref[t], b_ref[...])
+        found = dot(hidden[...], p_ref[outs * ch :]) + far0_ref[...]
+        far_out[:cols] = found
+        far_out[cols:] = jnp.zeros_like(far_out[cols:])
+        low = jnp.minimum(over_channels(jnp.min(found, axis=0, keepdims=True), jnp.minimum), near_ref[...])
+        high = jnp.maximum(over_channels(jnp.max(found, axis=0, keepdims=True), jnp.maximum), near_ref[...])
+        ends_ref[...] = jnp.where(lax.broadcasted_iota(jnp.int32, (8, lanes), 0) == 0, low, high)
+
+    return pl.pallas_call(
+        kernel,
+        in_specs=[IN_VMEM] * 6,
         out_specs=[IN_VMEM] * 2,
         out_shape=[pltpu.VMEM((cols + 8, lanes), F32), pltpu.VMEM((8, lanes), F32)],
-        scratch_shapes=[pltpu.VMEM((cols, clips * outs * ch), BF16)],
-        compiler_params=params(16),
-        cost_estimate=cost(cols * clips * outs * ch * lanes, 2 * 10**6),
-    )(*args)
+        scratch_shapes=[pltpu.VMEM((cols, outs * ch), BF16)],
+        compiler_params=params(16),
+    )(sums, far1, bias, placed, far_latents0, near_ends)
 
 
 def latent_messages(near, far, ends, other_ends, shards, copies):
@@ -315,13 +357,15 @@
         pairs = [(i, i + 1) for i in range(first, shards - 1, 2)]
         return lax.ppermute(x, "sp", pairs + [(b, a) for a, b in pairs])
 
-    near_sums, far_sums, near_taps, far_taps, inner_w, placed = edge_sums(frames, conv_weight, projection.T)
-    near, far = swap(near_sums, 0), swap(far_sums, 1)
-    sums = inner_sums(near_taps, far_taps, inner_w)
+    near_sums, far_sums0, near_taps, far_taps0, x1, far_w, inner, placed = first_edges(frames, conv_weight, projection.T)
+    near, far0 = swap(near_sums, 0), swap(far_sums0, 1)
+    far_sums1, far_taps1 = last_edges(x1, far_w)
+    far1 = swap(far_sums1, 1)
+    sums = inner_sums(near_taps, (far_taps0, far_taps1), inner)
 
     bias = conv_bias.reshape(1, ch)
-    near_latents, near_ends = row_latents(sums, 0, near, bias, placed)
-    far_latents, ends = row_latents(sums, 1, far, bias, placed, near_ends)
+    near_latents, far_latents0, near_ends = first_latents(sums, near, far0, bias, placed)
+    far_latents, ends = last_latents(sums, far1, bias, placed, far_latents0, near_ends)
     other_ends = lax.ppermute(ends, "grp", [(i, i ^ 1) for i in range(groups)])
     messages = latent_messages(near_latents, far_latents, ends, other_ends, shards, groups // 2)
     messages = messages.reshape(groups // 2 * shards, 16, messages.shape[-1])

time: 57.7 us -> 56.1 us (0.972)
  waiting for transfers between devices: 5.97 us -> 3.5 us
  starting transfers between devices: 2.89 us -> 3.54 us
    ppermute x2 -> x3, waiting for transfers between devices: 4.79 us -> 2.32 us  [swap(): return lax.ppermute(x, 'sp', pairs + [(b, a) for a, b in pairs])]
    ppermute x2 -> x3, starting transfers between devices: 2.89 us -> 3.53 us  [swap(): return lax.ppermute(x, 'sp', pairs + [(b, a) for a, b in pairs])]
    pallas_call x4 -> x5, Pallas kernels: 22 us -> 22.3 us  [the longest x1 10.8 us: inner_sums(): pl.pallas_call(kernel, in_specs=[IN_VMEM] * 4, out_specs=IN_VMEM, out_sha...]
  transfers between devices with their start and end apart: 3 -> 4, of which waited for: 2 -> 2; matrix products, arithmetic and copies ran while one was open for 0% -> 0% of each run, Pallas kernels for 20% -> 24%
where the time goes in v2:
time: 56.1 us; the launch traced here: 55.9 us
  blocking collectives  25.1 us (45%)
  Pallas kernels  23.6 us (42%)
  starting transfers between devices  3.54 us (6%)
  waiting for transfers between devices  3.5 us (6%)
    all_to_all x1, blocking collectives, on_device(): lax.all_to_all(messages, ('grp', 'sp'), 0, 0, axis_index_groups=same_core)  25.1 us
    pallas_call x1, Pallas kernels, inner_sums(): pl.pallas_call(kernel, in_specs=[IN_VMEM] * 4, out_specs=IN_VMEM, out_sha...  10.8 us
    pallas_call x1, Pallas kernels, first_edges(): pl.pallas_call(kernel, in_specs=[IN_HBM] * 3, out_specs=[IN_VMEM] * 8, ou...  8.21 us
    ppermute x3, starting transfers between devices, swap(): return lax.ppermute(x, 'sp', pairs + [(b, a) for a, b in pairs])  3.53 us
    ppermute x3, waiting for transfers between devices, swap(): return lax.ppermute(x, 'sp', pairs + [(b, a) for a, b in pairs])  2.32 us
    pallas_call x1, Pallas kernels, last_edges(): pl.pallas_call(kernel, in_specs=[IN_VMEM] * 2, out_specs=[IN_VMEM] * 2, o...  1.78 us
    pallas_call x1, Pallas kernels, coded_columns(): pl.pallas_call(kernel, in_specs=[IN_VMEM], out_specs=IN_VMEM, out_shape=j...  1.31 us
    ppermute x1, waiting for transfers between devices, on_device(): other_ends = lax.ppermute(ends, 'grp', [(i, i ^ 1) for i in range(groups)])  1.18 us
  transfers between devices with their start and end apart: 4, of which 2 were waited for; matrix products, arithmetic and copies ran while one was open for 0% of the time, Pallas kernels for 24%

profile of v2, /device:TPU:0, one launch (start us, length us, event | category | flops | bytes accessed | tf_op | source)
XLA Modules:
  0.0 55.9 jit_solution(17116854838716228561)
XLA Ops:
  0.0 8.2 %shard_map.46 = (bf16[2,2,240,384]{3,2,1,0:T(8,128)(2,1)S(1)}, bf16[2,240,384]{2,1,0:T(8,128)(2,1)S(1)}, bf16[2,240,4608]{2,1,0:T(8,128)(2,1)S(1)}, bf16[240,460...) custom-call(bf16[2,4,2,240,384]{4,3,2,1,0:T(8,128)(2,1)} %x_hbm.1, ...), custom_call_target="tpu_custom_call" | custom-call | tf_op jit(solution)/shard_map/pallas_call | solution.py:128
  8.2 0.0 copy-start
  8.2 2.0 %collective-permute-start = (bf16[2,2,240,384]{3,2,1,0:T(8,128)(2,1)S(1)}, bf16[2,2,240,384]{3,2,1,0:T(8,128)(2,1)S(1)}, u32[]{:S(2)}, u32[]{:S(2)}) collective-permute-start(bf16[2,2,240,384]{3,2,1,0:T(8,128)(2,1)S(1)} %get-tuple-element.26), channel_id=1, source_target_pairs={{0,1},{2,3},{4,5},{6,7},{8,9},{10,11},{12,13},{14,15},{1,0},{3,2},... | collective-permute-start | bytes 2211848 | tf_op jit(solution)/shard_map/ppermute | solution.py:358
  10.2 0.7 %collective-permute-start.1 = (bf16[2,240,384]{2,1,0:T(8,128)(2,1)S(1)}, bf16[2,240,384]{2,1,0:T(8,128)(2,1)S(1)}, u32[]{:S(2)}, u32[]{:S(2)}) collective-permute-start(bf16[2,240,384]{2,1,0:T(8,128)(2,1)S(1)} %get-tuple-element.27), channel_id=1, source_target_pairs={{1,2},{3,4},{5,6},{7,8},{9,10},{11,12},{13,14},{2,1},{4,3},{6,5},{... | collective-permute-start | bytes 1105928 | tf_op jit(solution)/shard_map/ppermute | solution.py:358
  10.9 1.8 %shard_map.47 = (bf16[2,240,384]{2,1,0:T(8,128)(2,1)S(1)}, bf16[240,4608]{1,0:T(8,128)(2,1)S(1)}) custom-call(bf16[4,240,384]{2,1,0:T(8,128)(2,1)S(1)} %get-tuple-element.22.x, bf16[3,384,1152]{2,1,0:T(8,128)(2,1)S(1)} %get-tuple-element.23.w), custom_call_target="tpu_custom_call" | custom-call | tf_op jit(solution)/shard_map/pallas_call | solution.py:163
  12.7 0.9 %collective-permute-start.2 = (bf16[2,240,384]{2,1,0:T(8,128)(2,1)S(1)}, bf16[2,240,384]{2,1,0:T(8,128)(2,1)S(1)}, u32[]{:S(2)}, u32[]{:S(2)}) collective-permute-start(bf16[2,240,384]{2,1,0:T(8,128)(2,1)S(1)} %get-tuple-element.30), channel_id=1, source_target_pairs={{1,2},{3,4},{5,6},{7,8},{9,10},{11,12},{13,14},{2,1},{4,3},{6,5},{... | collective-permute-start | bytes 1105928 | tf_op jit(solution)/shard_map/ppermute | solution.py:358
  13.6 0.0 copy-done
  13.6 10.8 %shard_map.48.s_ref = f32[2,2,240,768]{3,2,1,0:T(8,128)S(1)} custom-call(bf16[2,240,4608]{2,1,0:T(8,128)(2,1)S(1)} %get-tuple-element.20.near, bf16[240,4608]{1,0:T(8,128)(2,1)S(1)} %get-tuple-element.21.far0, bf16[240,4608]{1,0:T(8,128)(2,1)S(1)} %get-tuple-element.24.far1, bf16[3,3,384,1152]{3,2,1,0:T(8,128)(2,1)S(1)} %get-tuple-element.25.w), custom_call_target="tpu_custom_call" | custom-call | tf_op jit(solution)/shard_map/pallas_call | solution.py:184
  24.4 0.0 collective-permute-done.1.far0_ref
  24.4 2.3 %collective-permute-done.near_ref = bf16[2,2,240,384]{3,2,1,0:T(8,128)(2,1)S(1)} collective-permute-done((bf16[2,2,240,384]{3,2,1,0:T(8,128)(2,1)S(1)}, bf16[2,2,240,384]{3,2,1,0:T(8,128)(2,1)S(1)}, u32[]{:S(2)}, u32[]{:S(2)}) %collective-permute-start) | collective-permute-done | bytes 737312 | tf_op jit(solution)/shard_map/ppermute | solution.py:358
  26.7 1.0 %shard_map.49 = (f32[248,128]{1,0:T(8,128)S(1)}, f32[240,128]{1,0:T(8,128)S(1)}, f32[8,128]{1,0:T(8,128)S(1)}) custom-call(f32[2,2,240,768]{3,2,1,0:T(8,128)S(1)} %shard_map.48.s_ref, bf16[2,2,240,384]{3,2,1,0:T(8,128)(2,1)S(1)} %collective-permute-done.near_ref, bf16[2,240,384]{2,1,0:T(8,128)(2,1)S(1)} %collective-permute-done.1.far0_ref, ...), custom_call_target="tpu_custom_call" | custom-call | tf_op jit(solution)/shard_map/pallas_call | solution.py:224
  27.7 0.0 collective-permute-done.2.far1_ref
  27.7 0.5 shard_map.50
  28.2 0.0 collective-permute-start.3
  28.2 1.2 %collective-permute-done.3.other_ref = f32[8,128]{1,0:T(8,128)S(1)} collective-permute-done((f32[8,128]{1,0:T(8,128)S(1)}, f32[8,128]{1,0:T(8,128)S(1)}, u32[]{:S(2)}, u32[]{:S(2)}) %collective-permute-start.3) | collective-permute-done | bytes 4128 | tf_op jit(solution)/shard_map/ppermute | solution.py:369
  29.4 0.1 shard_map.51
  29.4 25.1 %all_to_all.5 = bf16[64,16,128]{2,1,0:T(8,128)(2,1)S(1)} all-to-all(bf16[64,16,128]{2,1,0:T(8,128)(2,1)S(1)} %bitcast.6), channel_id=1, replica_groups={{0,1,2,3,4,5,6,7,8,9,10,11,12,13,14,15,32,33,34,35,36,37,38,39,40,41,42..., dimensions={0} | all-to-all | bytes 524288 | tf_op jit(solution)/shard_map/all_to_all | solution.py:373
  54.6 1.3 %shard_map.52 = bf16[960,32]{1,0:T(8,128)(2,1)} custom-call(bf16[4,16,16,128]{3,2,1,0:T(8,128)(2,1)S(1)} %bitcast.7), custom_call_target="tpu_custom_call" | custom-call | tf_op jit(solution)/shard_map/pallas_call | solution.py:339
  (1 shorter events, 0.0 us)
Async XLA Ops:
  8.2 5.4 %copy-start = (f32[384]{0:T(512)S(1)}, f32[384]{0:T(512)}, u32[]{:S(2)}) copy-start(f32[384]{0:T(512)} %param.6) | copy-start | bytes 4612
  8.2 18.5 %collective-permute-start = (bf16[2,2,240,384]{3,2,1,0:T(8,128)(2,1)S(1)}, bf16[2,2,240,384]{3,2,1,0:T(8,128)(2,1)S(1)}, u32[]{:S(2)}, u32[]{:S(2)}) collective-permute-start(bf16[2,2,240,384]{3,2,1,0:T(8,128)(2,1)S(1)} %get-tuple-element.26), channel_id=1, source_target_pairs={{0,1},{2,3},{4,5},{6,7},{8,9},{10,11},{12,13},{14,15},{1,0},{3,2},... | collective-permute-start | bytes 2211848 | tf_op jit(solution)/shard_map/ppermute | solution.py:358
  10.2 14.2 %collective-permute-start.1 = (bf16[2,240,384]{2,1,0:T(8,128)(2,1)S(1)}, bf16[2,240,384]{2,1,0:T(8,128)(2,1)S(1)}, u32[]{:S(2)}, u32[]{:S(2)}) collective-permute-start(bf16[2,240,384]{2,1,0:T(8,128)(2,1)S(1)} %get-tuple-element.27), channel_id=1, source_target_pairs={{1,2},{3,4},{5,6},{7,8},{9,10},{11,12},{13,14},{2,1},{4,3},{6,5},{... | collective-permute-start | bytes 1105928 | tf_op jit(solution)/shard_map/ppermute | solution.py:358
  12.7 15.0 %collective-permute-start.2 = (bf16[2,240,384]{2,1,0:T(8,128)(2,1)S(1)}, bf16[2,240,384]{2,1,0:T(8,128)(2,1)S(1)}, u32[]{:S(2)}, u32[]{:S(2)}) collective-permute-start(bf16[2,240,384]{2,1,0:T(8,128)(2,1)S(1)} %get-tuple-element.30), channel_id=1, source_target_pairs={{1,2},{3,4},{5,6},{7,8},{9,10},{11,12},{13,14},{2,1},{4,3},{6,5},{... | collective-permute-start | bytes 1105928 | tf_op jit(solution)/shard_map/ppermute | solution.py:358
  28.2 1.2 %collective-permute-start.3 = (f32[8,128]{1,0:T(8,128)S(1)}, f32[8,128]{1,0:T(8,128)S(1)}, u32[]{:S(2)}, u32[]{:S(2)}) collective-permute-start(f32[8,128]{1,0:T(8,128)S(1)} %get-tuple-element.34.e_ref), channel_id=1, source_target_pairs={{0,16},{16,0},{32,48},{48,32},{64,80},{80,64},{96,112},{112,96},{1... | collective-permute-start | bytes 12296 | tf_op jit(solution)/shard_map/ppermute | solution.py:369

commit v3 on v2

--- a/solution.py
+++ b/solution.py
@@ -201,59 +201,52 @@
     return (h + h * jnp.tanh(h)).astype(BF16)
 
 
-def first_latents(sums, near, far0, bias, placed):
+def arrival(halo):
+    def kernel(x_ref, o_ref):
+        o_ref[...] = x_ref[0, :16, :128].astype(F32)
+
+    return pl.pallas_call(
+        kernel,
+        in_specs=[IN_VMEM],
+        out_specs=IN_VMEM,
+        out_shape=pltpu.VMEM((16, 128), F32),
+        compiler_params=params(16),
+        cost_estimate=cost(27 * 10**8, 10**3),
+    )(halo)
+
+
+def row_latents(sums, part, halos, bias, placed, other_ends, token):
     clips, outs, cols, wide = sums.shape
     ch = wide // 2
     lanes = placed.shape[1]
-
-    def kernel(s_ref, near_ref, far0_ref, b_ref, p_ref, near_out, far_out, ends_ref, hidden):
+    extra = [x for x in (other_ends, token) if x is not None]
+
+    def kernel(s_ref, b_ref, p_ref, *refs):
+        halo_refs, (o_ref, ends_ref, hidden) = refs[: len(halos)], refs[-3:]
         for c in range(clips):
             for t in range(outs):
+                halo = halo_refs[c][t] if len(halos) == clips else halo_refs[0][c, t]
                 at = (c * outs + t) * ch
-                hidden[0, :, at : at + ch] = hidden_units(s_ref[c, t, :, :ch], near_ref[c, t], b_ref[...])
-        for t in range(outs):
-            hidden[1, :, t * ch : (t + 1) * ch] = hidden_units(s_ref[0, t, :, ch:], far0_ref[t], b_ref[...])
-        found = dot(hidden[0], p_ref[...])
-        near_out[:cols] = found
-        near_out[cols:] = jnp.zeros_like(near_out[cols:])
-        far_out[...] = dot(hidden[1, :, : outs * ch], p_ref[: outs * ch])
+                hidden[:, at : at + ch] = hidden_units(s_ref[c, t, :, part * ch : (part + 1) * ch], halo, b_ref[...])
+        found = dot(hidden[...], p_ref[...])
+        o_ref[:cols] = found
+        o_ref[cols:] = jnp.zeros_like(o_ref[cols:])
         low = over_channels(jnp.min(found, axis=0, keepdims=True), jnp.minimum)
         high = over_channels(jnp.max(found, axis=0, keepdims=True), jnp.maximum)
+        if other_ends is not None:
+            other = refs[len(halos)]
+            low, high = jnp.minimum(low, other[...]), jnp.maximum(high, other[...])
         ends_ref[...] = jnp.where(lax.broadcasted_iota(jnp.int32, (8, lanes), 0) == 0, low, high)
 
-    return pl.pallas_call(
-        kernel,
-        in_specs=[IN_VMEM] * 5,
-        out_specs=[IN_VMEM] * 3,
-        out_shape=[pltpu.VMEM((cols + 8, lanes), F32), pltpu.VMEM((cols, lanes), F32), pltpu.VMEM((8, lanes), F32)],
-        scratch_shapes=[pltpu.VMEM((2, cols, clips * outs * ch), BF16)],
-        compiler_params=params(16),
-    )(sums, near, far0, bias, placed)
-
-
-def last_latents(sums, far1, bias, placed, far_latents0, near_ends):
-    clips, outs, cols, wide = sums.shape
-    ch = wide // 2
-    lanes = placed.shape[1]
-
-    def kernel(s_ref, far1_ref, b_ref, p_ref, far0_ref, near_ref, far_out, ends_ref, hidden):
-        for t in range(outs):
-            hidden[:, t * ch : (t + 1) * ch] = hidden_units(s_ref[1, t, :, ch:], far1_ref[t], b_ref[...])
-        found = dot(hidden[...], p_ref[outs * ch :]) + far0_ref[...]
-        far_out[:cols] = found
-        far_out[cols:] = jnp.zeros_like(far_out[cols:])
-        low = jnp.minimum(over_channels(jnp.min(found, axis=0, keepdims=True), jnp.minimum), near_ref[...])
-        high = jnp.maximum(over_channels(jnp.max(found, axis=0, keepdims=True), jnp.maximum), near_ref[...])
-        ends_ref[...] = jnp.where(lax.broadcasted_iota(jnp.int32, (8, lanes), 0) == 0, low, high)
-
-    return pl.pallas_call(
-        kernel,
-        in_specs=[IN_VMEM] * 6,
+    args = [sums, bias, placed, *halos, *extra]
+    return pl.pallas_call(
+        kernel,
+        in_specs=[IN_VMEM] * len(args),
         out_specs=[IN_VMEM] * 2,
         out_shape=[pltpu.VMEM((cols + 8, lanes), F32), pltpu.VMEM((8, lanes), F32)],
-        scratch_shapes=[pltpu.VMEM((cols, outs * ch), BF16)],
-        compiler_params=params(16),
-    )(sums, far1, bias, placed, far_latents0, near_ends)
+        scratch_shapes=[pltpu.VMEM((cols, clips * outs * ch), BF16)],
+        compiler_params=params(16),
+    )(*args)
 
 
 def latent_messages(near, far, ends, other_ends, shards, copies):
@@ -364,8 +357,8 @@
     sums = inner_sums(near_taps, (far_taps0, far_taps1), inner)
 
     bias = conv_bias.reshape(1, ch)
-    near_latents, far_latents0, near_ends = first_latents(sums, near, far0, bias, placed)
-    far_latents, ends = last_latents(sums, far1, bias, placed, far_latents0, near_ends)
+    far_latents, far_ends = row_latents(sums, 1, (far0, far1), bias, placed, None, arrival(far0))
+    near_latents, ends = row_latents(sums, 0, (near,), bias, placed, far_ends, None)
     other_ends = lax.ppermute(ends, "grp", [(i, i ^ 1) for i in range(groups)])
     messages = latent_messages(near_latents, far_latents, ends, other_ends, shards, groups // 2)
     messages = messages.reshape(groups // 2 * shards, 16, messages.shape[-1])

time: 56.1 us -> 57 us (1.016)
  starting transfers between devices: 3.54 us -> 6.77 us
  blocking collectives: 25.1 us -> 23 us
    ppermute x3, starting transfers between devices: 3.53 us -> 6.77 us  [swap(): return lax.ppermute(x, 'sp', pairs + [(b, a) for a, b in pairs])]
    all_to_all x1, blocking collectives: 25.1 us -> 23 us  [on_device(): lax.all_to_all(messages, ('grp', 'sp'), 0, 0, axis_index_groups=same_core)]
    pallas_call x2 -> x3, Pallas kernels: 1.49 us -> 1.62 us  [the longest x2 1.61 us: row_latents(): pl.pallas_call(kernel, in_specs=[IN_VMEM] * len(args), out_specs=[IN_VMEM...]
where the time goes in v3:
time: 57 us; the launch traced here: 56.7 us
  Pallas kernels  23.8 us (42%)
  blocking collectives  23 us (40%)
  starting transfers between devices  6.77 us (12%)
  waiting for transfers between devices  3.08 us (5%)
    all_to_all x1, blocking collectives, on_device(): lax.all_to_all(messages, ('grp', 'sp'), 0, 0, axis_index_groups=same_core)  23 us
    pallas_call x1, Pallas kernels, inner_sums(): pl.pallas_call(kernel, in_specs=[IN_VMEM] * 4, out_specs=IN_VMEM, out_sha...  10.8 us
    pallas_call x1, Pallas kernels, first_edges(): pl.pallas_call(kernel, in_specs=[IN_HBM] * 3, out_specs=[IN_VMEM] * 8, ou...  8.21 us
    ppermute x3, starting transfers between devices, swap(): return lax.ppermute(x, 'sp', pairs + [(b, a) for a, b in pairs])  6.77 us
    ppermute x3, waiting for transfers between devices, swap(): return lax.ppermute(x, 'sp', pairs + [(b, a) for a, b in pairs])  1.9 us
    pallas_call x1, Pallas kernels, last_edges(): pl.pallas_call(kernel, in_specs=[IN_VMEM] * 2, out_specs=[IN_VMEM] * 2, o...  1.78 us
    pallas_call x2, Pallas kernels, row_latents(): pl.pallas_call(kernel, in_specs=[IN_VMEM] * len(args), out_specs=[IN_VMEM...  1.61 us
    pallas_call x1, Pallas kernels, coded_columns(): pl.pallas_call(kernel, in_specs=[IN_VMEM], out_specs=IN_VMEM, out_shape=j...  1.31 us
  transfers between devices with their start and end apart: 4, of which 2 were waited for; matrix products, arithmetic and copies ran while one was open for 0% of the time, Pallas kernels for 24%

profile of v3, /device:TPU:0, one launch (start us, length us, event | category | flops | bytes accessed | tf_op | source)
XLA Modules:
  0.0 56.7 jit_solution(6674417771291488454)
XLA Ops:
  0.0 8.2 %shard_map.46 = (bf16[2,2,240,384]{3,2,1,0:T(8,128)(2,1)S(1)}, bf16[2,240,384]{2,1,0:T(8,128)(2,1)S(1)}, bf16[2,240,4608]{2,1,0:T(8,128)(2,1)S(1)}, bf16[240,460...) custom-call(bf16[2,4,2,240,384]{4,3,2,1,0:T(8,128)(2,1)} %x_hbm.1, ...), custom_call_target="tpu_custom_call" | custom-call | tf_op jit(solution)/shard_map/pallas_call | solution.py:128
  8.2 0.0 copy-start
  8.2 0.7 %collective-permute-start.1 = (bf16[2,240,384]{2,1,0:T(8,128)(2,1)S(1)}, bf16[2,240,384]{2,1,0:T(8,128)(2,1)S(1)}, u32[]{:S(2)}, u32[]{:S(2)}) collective-permute-start(bf16[2,240,384]{2,1,0:T(8,128)(2,1)S(1)} %get-tuple-element.27), channel_id=1, source_target_pairs={{1,2},{3,4},{5,6},{7,8},{9,10},{11,12},{13,14},{2,1},{4,3},{6,5},{... | collective-permute-start | bytes 1105928 | tf_op jit(solution)/shard_map/ppermute | solution.py:351
  8.9 5.2 %collective-permute-start = (bf16[2,2,240,384]{3,2,1,0:T(8,128)(2,1)S(1)}, bf16[2,2,240,384]{3,2,1,0:T(8,128)(2,1)S(1)}, u32[]{:S(2)}, u32[]{:S(2)}) collective-permute-start(bf16[2,2,240,384]{3,2,1,0:T(8,128)(2,1)S(1)} %get-tuple-element.26), channel_id=1, source_target_pairs={{0,1},{2,3},{4,5},{6,7},{8,9},{10,11},{12,13},{14,15},{1,0},{3,2},... | collective-permute-start | bytes 2211848 | tf_op jit(solution)/shard_map/ppermute | solution.py:351
  14.1 1.8 %shard_map.47 = (bf16[2,240,384]{2,1,0:T(8,128)(2,1)S(1)}, bf16[240,4608]{1,0:T(8,128)(2,1)S(1)}) custom-call(bf16[4,240,384]{2,1,0:T(8,128)(2,1)S(1)} %get-tuple-element.21.x, bf16[3,384,1152]{2,1,0:T(8,128)(2,1)S(1)} %get-tuple-element.22.w), custom_call_target="tpu_custom_call" | custom-call | tf_op jit(solution)/shard_map/pallas_call | solution.py:163
  15.9 0.9 %collective-permute-start.2 = (bf16[2,240,384]{2,1,0:T(8,128)(2,1)S(1)}, bf16[2,240,384]{2,1,0:T(8,128)(2,1)S(1)}, u32[]{:S(2)}, u32[]{:S(2)}) collective-permute-start(bf16[2,240,384]{2,1,0:T(8,128)(2,1)S(1)} %get-tuple-element.28), channel_id=1, source_target_pairs={{1,2},{3,4},{5,6},{7,8},{9,10},{11,12},{13,14},{2,1},{4,3},{6,5},{... | collective-permute-start | bytes 1105928 | tf_op jit(solution)/shard_map/ppermute | solution.py:351
  16.8 0.0 copy-done
  16.8 10.8 %shard_map.48.s_ref = f32[2,2,240,768]{3,2,1,0:T(8,128)S(1)} custom-call(bf16[2,240,4608]{2,1,0:T(8,128)(2,1)S(1)} %get-tuple-element.19.near, bf16[240,4608]{1,0:T(8,128)(2,1)S(1)} %get-tuple-element.20.far0, bf16[240,4608]{1,0:T(8,128)(2,1)S(1)} %get-tuple-element.23.far1, bf16[3,3,384,1152]{3,2,1,0:T(8,128)(2,1)S(1)} %get-tuple-element.24.w), custom_call_target="tpu_custom_call" | custom-call | tf_op jit(solution)/shard_map/pallas_call | solution.py:184
  27.6 0.0 collective-permute-done.1.x_ref.refs_0_
  27.6 0.0 collective-permute-done.2.refs_1_
  27.6 0.8 %shard_map.50 = (f32[248,128]{1,0:T(8,128)S(1)}, f32[8,128]{1,0:T(8,128)S(1)}) custom-call(f32[2,2,240,768]{3,2,1,0:T(8,128)S(1)} %shard_map.48.s_ref, f32[1,384]{1,0:T(1,128)S(1)} %reshape.12.b_ref, bf16[1536,128]{1,0:T(8,128)(2,1)S(1)} %get-tuple-element.25.p_ref, bf16[2,240,384]{2,1,0:T(8,128)(2,1)S(1)} %collective-permute-done.1.x_ref.refs_0_, ...), custom_call_target="tpu_custom_call" | custom-call | tf_op jit(solution)/shard_map/pallas_call | solution.py:242
  28.4 1.9 %collective-permute-done.refs_0_ = bf16[2,2,240,384]{3,2,1,0:T(8,128)(2,1)S(1)} collective-permute-done((bf16[2,2,240,384]{3,2,1,0:T(8,128)(2,1)S(1)}, bf16[2,2,240,384]{3,2,1,0:T(8,128)(2,1)S(1)}, u32[]{:S(2)}, u32[]{:S(2)}) %collective-permute-start) | collective-permute-done | bytes 737312 | tf_op jit(solution)/shard_map/ppermute | solution.py:351
  30.3 0.8 %shard_map.51 = (f32[248,128]{1,0:T(8,128)S(1)}, f32[8,128]{1,0:T(8,128)S(1)}) custom-call(f32[2,2,240,768]{3,2,1,0:T(8,128)S(1)} %shard_map.48.s_ref, f32[1,384]{1,0:T(1,128)S(1)} %reshape.12.b_ref, bf16[1536,128]{1,0:T(8,128)(2,1)S(1)} %get-tuple-element.25.p_ref, bf16[2,2,240,384]{3,2,1,0:T(8,128)(2,1)S(1)} %collective-permute-done.refs_0_, ...), custom_call_target="tpu_custom_call" | custom-call | tf_op jit(solution)/shard_map/pallas_call | solution.py:242
  31.2 0.0 collective-permute-start.3
  31.2 1.2 %collective-permute-done.3.other_ref = f32[8,128]{1,0:T(8,128)S(1)} collective-permute-done((f32[8,128]{1,0:T(8,128)S(1)}, f32[8,128]{1,0:T(8,128)S(1)}, u32[]{:S(2)}, u32[]{:S(2)}) %collective-permute-start.3) | collective-permute-done | bytes 4128 | tf_op jit(solution)/shard_map/ppermute | solution.py:362
  32.3 0.1 shard_map.52
  32.4 23.0 %all_to_all.5 = bf16[64,16,128]{2,1,0:T(8,128)(2,1)S(1)} all-to-all(bf16[64,16,128]{2,1,0:T(8,128)(2,1)S(1)} %bitcast.6), channel_id=1, replica_groups={{0,1,2,3,4,5,6,7,8,9,10,11,12,13,14,15,32,33,34,35,36,37,38,39,40,41,42..., dimensions={0} | all-to-all | bytes 524288 | tf_op jit(solution)/shard_map/all_to_all | solution.py:366
  55.4 1.3 %shard_map.53 = bf16[960,32]{1,0:T(8,128)(2,1)} custom-call(bf16[4,16,16,128]{3,2,1,0:T(8,128)(2,1)S(1)} %bitcast.7), custom_call_target="tpu_custom_call" | custom-call | tf_op jit(solution)/shard_map/pallas_call | solution.py:332
  (2 shorter events, 0.0 us)
Async XLA Ops:
  8.2 8.6 %copy-start = (f32[384]{0:T(512)S(1)}, f32[384]{0:T(512)}, u32[]{:S(2)}) copy-start(f32[384]{0:T(512)} %param.6) | copy-start | bytes 4612
  8.2 19.4 %collective-permute-start.1 = (bf16[2,240,384]{2,1,0:T(8,128)(2,1)S(1)}, bf16[2,240,384]{2,1,0:T(8,128)(2,1)S(1)}, u32[]{:S(2)}, u32[]{:S(2)}) collective-permute-start(bf16[2,240,384]{2,1,0:T(8,128)(2,1)S(1)} %get-tuple-element.27), channel_id=1, source_target_pairs={{1,2},{3,4},{5,6},{7,8},{9,10},{11,12},{13,14},{2,1},{4,3},{6,5},{... | collective-permute-start | bytes 1105928 | tf_op jit(solution)/shard_map/ppermute | solution.py:351
  8.9 21.4 %collective-permute-start = (bf16[2,2,240,384]{3,2,1,0:T(8,128)(2,1)S(1)}, bf16[2,2,240,384]{3,2,1,0:T(8,128)(2,1)S(1)}, u32[]{:S(2)}, u32[]{:S(2)}) collective-permute-start(bf16[2,2,240,384]{3,2,1,0:T(8,128)(2,1)S(1)} %get-tuple-element.26), channel_id=1, source_target_pairs={{0,1},{2,3},{4,5},{6,7},{8,9},{10,11},{12,13},{14,15},{1,0},{3,2},... | collective-permute-start | bytes 2211848 | tf_op jit(solution)/shard_map/ppermute | solution.py:351
  15.9 11.7 %collective-permute-start.2 = (bf16[2,240,384]{2,1,0:T(8,128)(2,1)S(1)}, bf16[2,240,384]{2,1,0:T(8,128)(2,1)S(1)}, u32[]{:S(2)}, u32[]{:S(2)}) collective-permute-start(bf16[2,240,384]{2,1,0:T(8,128)(2,1)S(1)} %get-tuple-element.28), channel_id=1, source_target_pairs={{1,2},{3,4},{5,6},{7,8},{9,10},{11,12},{13,14},{2,1},{4,3},{6,5},{... | collective-permute-start | bytes 1105928 | tf_op jit(solution)/shard_map/ppermute | solution.py:351
  31.2 1.2 %collective-permute-start.3 = (f32[8,128]{1,0:T(8,128)S(1)}, f32[8,128]{1,0:T(8,128)S(1)}, u32[]{:S(2)}, u32[]{:S(2)}) collective-permute-start(f32[8,128]{1,0:T(8,128)S(1)} %get-tuple-element.32.e_ref), channel_id=1, source_target_pairs={{0,16},{16,0},{32,48},{48,32},{64,80},{80,64},{96,112},{112,96},{1... | collective-permute-start | bytes 12296 | tf_op jit(solution)/shard_map/ppermute | solution.py:362

commit v4 on v2

--- a/solution.py
+++ b/solution.py
@@ -201,12 +201,26 @@
     return (h + h * jnp.tanh(h)).astype(BF16)
 
 
-def first_latents(sums, near, far0, bias, placed):
+def arrival(halo):
+    def kernel(x_ref, o_ref):
+        o_ref[...] = x_ref[0, :16, :128].astype(F32)
+
+    return pl.pallas_call(
+        kernel,
+        in_specs=[IN_VMEM],
+        out_specs=IN_VMEM,
+        out_shape=pltpu.VMEM((16, 128), F32),
+        compiler_params=params(16),
+        cost_estimate=cost(27 * 10**8, 10**3),
+    )(halo)
+
+
+def first_latents(sums, near, far0, bias, placed, token):
     clips, outs, cols, wide = sums.shape
     ch = wide // 2
     lanes = placed.shape[1]
 
-    def kernel(s_ref, near_ref, far0_ref, b_ref, p_ref, near_out, far_out, ends_ref, hidden):
+    def kernel(s_ref, near_ref, far0_ref, b_ref, p_ref, _, near_out, far_out, ends_ref, hidden):
         for c in range(clips):
             for t in range(outs):
                 at = (c * outs + t) * ch
@@ -223,12 +237,12 @@
 
     return pl.pallas_call(
         kernel,
-        in_specs=[IN_VMEM] * 5,
+        in_specs=[IN_VMEM] * 6,
         out_specs=[IN_VMEM] * 3,
         out_shape=[pltpu.VMEM((cols + 8, lanes), F32), pltpu.VMEM((cols, lanes), F32), pltpu.VMEM((8, lanes), F32)],
         scratch_shapes=[pltpu.VMEM((2, cols, clips * outs * ch), BF16)],
         compiler_params=params(16),
-    )(sums, near, far0, bias, placed)
+    )(sums, near, far0, bias, placed, token)
 
 
 def last_latents(sums, far1, bias, placed, far_latents0, near_ends):
@@ -364,7 +378,7 @@
     sums = inner_sums(near_taps, (far_taps0, far_taps1), inner)
 
     bias = conv_bias.reshape(1, ch)
-    near_latents, far_latents0, near_ends = first_latents(sums, near, far0, bias, placed)
+    near_latents, far_latents0, near_ends = first_latents(sums, near, far0, bias, placed, arrival(far0))
     far_latents, ends = last_latents(sums, far1, bias, placed, far_latents0, near_ends)
     other_ends = lax.ppermute(ends, "grp", [(i, i ^ 1) for i in range(groups)])
     messages = latent_messages(near_latents, far_latents, ends, other_ends, shards, groups // 2)

time: 56.1 us -> 55.9 us (level)
  blocking collectives: 25.1 us -> 21.2 us
  starting transfers between devices: 3.54 us -> 6.77 us
    all_to_all x1, blocking collectives: 25.1 us -> 21.2 us  [on_device(): lax.all_to_all(messages, ('grp', 'sp'), 0, 0, axis_index_groups=same_core)]
    ppermute x3, starting transfers between devices: 3.53 us -> 6.77 us  [swap(): return lax.ppermute(x, 'sp', pairs + [(b, a) for a, b in pairs])]
where the time goes in v4:
time: 55.9 us; the launch traced here: 55.6 us
  Pallas kernels  23.6 us (42%)
  blocking collectives  21.2 us (38%)
  starting transfers between devices  6.77 us (12%)
  waiting for transfers between devices  3.89 us (7%)
    all_to_all x1, blocking collectives, on_device(): lax.all_to_all(messages, ('grp', 'sp'), 0, 0, axis_index_groups=same_core)  21.2 us
    pallas_call x1, Pallas kernels, inner_sums(): pl.pallas_call(kernel, in_specs=[IN_VMEM] * 4, out_specs=IN_VMEM, out_sha...  10.8 us
    pallas_call x1, Pallas kernels, first_edges(): pl.pallas_call(kernel, in_specs=[IN_HBM] * 3, out_specs=[IN_VMEM] * 8, ou...  8.21 us
    ppermute x3, starting transfers between devices, swap(): return lax.ppermute(x, 'sp', pairs + [(b, a) for a, b in pairs])  6.77 us
    ppermute x3, waiting for transfers between devices, swap(): return lax.ppermute(x, 'sp', pairs + [(b, a) for a, b in pairs])  2.72 us
    pallas_call x1, Pallas kernels, last_edges(): pl.pallas_call(kernel, in_specs=[IN_VMEM] * 2, out_specs=[IN_VMEM] * 2, o...  1.78 us
    pallas_call x1, Pallas kernels, coded_columns(): pl.pallas_call(kernel, in_specs=[IN_VMEM], out_specs=IN_VMEM, out_shape=j...  1.31 us
    ppermute x1, waiting for transfers between devices, on_device(): other_ends = lax.ppermute(ends, 'grp', [(i, i ^ 1) for i in range(groups)])  1.18 us
  transfers between devices with their start and end apart: 4, of which 2 were waited for; matrix products, arithmetic and copies ran while one was open for 0% of the time, Pallas kernels for 24%

profile of v4, /device:TPU:0, one launch (start us, length us, event | category | flops | bytes accessed | tf_op | source)
XLA Modules:
  0.0 55.6 jit_solution(5639282209710278426)
XLA Ops:
  0.0 8.2 %shard_map.46 = (bf16[2,2,240,384]{3,2,1,0:T(8,128)(2,1)S(1)}, bf16[2,240,384]{2,1,0:T(8,128)(2,1)S(1)}, bf16[2,240,4608]{2,1,0:T(8,128)(2,1)S(1)}, bf16[240,460...) custom-call(bf16[2,4,2,240,384]{4,3,2,1,0:T(8,128)(2,1)} %x_hbm.1, ...), custom_call_target="tpu_custom_call" | custom-call | tf_op jit(solution)/shard_map/pallas_call | solution.py:128
  8.2 0.0 copy-start
  8.2 0.7 %collective-permute-start.1 = (bf16[2,240,384]{2,1,0:T(8,128)(2,1)S(1)}, bf16[2,240,384]{2,1,0:T(8,128)(2,1)S(1)}, u32[]{:S(2)}, u32[]{:S(2)}) collective-permute-start(bf16[2,240,384]{2,1,0:T(8,128)(2,1)S(1)} %get-tuple-element.27), channel_id=1, source_target_pairs={{1,2},{3,4},{5,6},{7,8},{9,10},{11,12},{13,14},{2,1},{4,3},{6,5},{... | collective-permute-start | bytes 1105928 | tf_op jit(solution)/shard_map/ppermute | solution.py:372
  8.9 5.2 %collective-permute-start = (bf16[2,2,240,384]{3,2,1,0:T(8,128)(2,1)S(1)}, bf16[2,2,240,384]{3,2,1,0:T(8,128)(2,1)S(1)}, u32[]{:S(2)}, u32[]{:S(2)}) collective-permute-start(bf16[2,2,240,384]{3,2,1,0:T(8,128)(2,1)S(1)} %get-tuple-element.26), channel_id=1, source_target_pairs={{0,1},{2,3},{4,5},{6,7},{8,9},{10,11},{12,13},{14,15},{1,0},{3,2},... | collective-permute-start | bytes 2211848 | tf_op jit(solution)/shard_map/ppermute | solution.py:372
  14.1 1.8 %shard_map.47 = (bf16[2,240,384]{2,1,0:T(8,128)(2,1)S(1)}, bf16[240,4608]{1,0:T(8,128)(2,1)S(1)}) custom-call(bf16[4,240,384]{2,1,0:T(8,128)(2,1)S(1)} %get-tuple-element.22.x, bf16[3,384,1152]{2,1,0:T(8,128)(2,1)S(1)} %get-tuple-element.23.w), custom_call_target="tpu_custom_call" | custom-call | tf_op jit(solution)/shard_map/pallas_call | solution.py:163
  15.9 0.9 %collective-permute-start.2 = (bf16[2,240,384]{2,1,0:T(8,128)(2,1)S(1)}, bf16[2,240,384]{2,1,0:T(8,128)(2,1)S(1)}, u32[]{:S(2)}, u32[]{:S(2)}) collective-permute-start(bf16[2,240,384]{2,1,0:T(8,128)(2,1)S(1)} %get-tuple-element.30), channel_id=1, source_target_pairs={{1,2},{3,4},{5,6},{7,8},{9,10},{11,12},{13,14},{2,1},{4,3},{6,5},{... | collective-permute-start | bytes 1105928 | tf_op jit(solution)/shard_map/ppermute | solution.py:372
  16.8 0.0 copy-done
  16.8 10.8 %shard_map.48.s_ref = f32[2,2,240,768]{3,2,1,0:T(8,128)S(1)} custom-call(bf16[2,240,4608]{2,1,0:T(8,128)(2,1)S(1)} %get-tuple-element.20.near, bf16[240,4608]{1,0:T(8,128)(2,1)S(1)} %get-tuple-element.21.far0, bf16[240,4608]{1,0:T(8,128)(2,1)S(1)} %get-tuple-element.24.far1, bf16[3,3,384,1152]{3,2,1,0:T(8,128)(2,1)S(1)} %get-tuple-element.25.w), custom_call_target="tpu_custom_call" | custom-call | tf_op jit(solution)/shard_map/pallas_call | solution.py:184
  27.6 0.0 collective-permute-done.1.x_ref.far0_ref
  27.6 2.7 %collective-permute-done.near_ref = bf16[2,2,240,384]{3,2,1,0:T(8,128)(2,1)S(1)} collective-permute-done((bf16[2,2,240,384]{3,2,1,0:T(8,128)(2,1)S(1)}, bf16[2,2,240,384]{3,2,1,0:T(8,128)(2,1)S(1)}, u32[]{:S(2)}, u32[]{:S(2)}) %collective-permute-start) | collective-permute-done | bytes 737312 | tf_op jit(solution)/shard_map/ppermute | solution.py:372
  30.3 1.0 %shard_map.50 = (f32[248,128]{1,0:T(8,128)S(1)}, f32[240,128]{1,0:T(8,128)S(1)}, f32[8,128]{1,0:T(8,128)S(1)}) custom-call(f32[2,2,240,768]{3,2,1,0:T(8,128)S(1)} %shard_map.48.s_ref, bf16[2,2,240,384]{3,2,1,0:T(8,128)(2,1)S(1)} %collective-permute-done.near_ref, bf16[2,240,384]{2,1,0:T(8,128)(2,1)S(1)} %collective-permute-done.1.x_ref.far0_ref, ...), custom_call_target="tpu_custom_call" | custom-call | tf_op jit(solution)/shard_map/pallas_call | solution.py:238
  31.3 0.0 collective-permute-done.2.far1_ref
  31.3 0.5 shard_map.51
  31.8 0.0 collective-permute-start.3
  31.9 1.2 %collective-permute-done.3.other_ref = f32[8,128]{1,0:T(8,128)S(1)} collective-permute-done((f32[8,128]{1,0:T(8,128)S(1)}, f32[8,128]{1,0:T(8,128)S(1)}, u32[]{:S(2)}, u32[]{:S(2)}) %collective-permute-start.3) | collective-permute-done | bytes 4128 | tf_op jit(solution)/shard_map/ppermute | solution.py:383
  33.0 0.1 shard_map.52
  33.1 21.2 %all_to_all.5 = bf16[64,16,128]{2,1,0:T(8,128)(2,1)S(1)} all-to-all(bf16[64,16,128]{2,1,0:T(8,128)(2,1)S(1)} %bitcast.6), channel_id=1, replica_groups={{0,1,2,3,4,5,6,7,8,9,10,11,12,13,14,15,32,33,34,35,36,37,38,39,40,41,42..., dimensions={0} | all-to-all | bytes 524288 | tf_op jit(solution)/shard_map/all_to_all | solution.py:387
  54.3 1.3 %shard_map.53 = bf16[960,32]{1,0:T(8,128)(2,1)} custom-call(bf16[4,16,16,128]{3,2,1,0:T(8,128)(2,1)S(1)} %bitcast.7), custom_call_target="tpu_custom_call" | custom-call | tf_op jit(solution)/shard_map/pallas_call | solution.py:353
  (2 shorter events, 0.0 us)
Async XLA Ops:
  8.2 8.6 %copy-start = (f32[384]{0:T(512)S(1)}, f32[384]{0:T(512)}, u32[]{:S(2)}) copy-start(f32[384]{0:T(512)} %param.6) | copy-start | bytes 4612
  8.2 19.4 %collective-permute-start.1 = (bf16[2,240,384]{2,1,0:T(8,128)(2,1)S(1)}, bf16[2,240,384]{2,1,0:T(8,128)(2,1)S(1)}, u32[]{:S(2)}, u32[]{:S(2)}) collective-permute-start(bf16[2,240,384]{2,1,0:T(8,128)(2,1)S(1)} %get-tuple-element.27), channel_id=1, source_target_pairs={{1,2},{3,4},{5,6},{7,8},{9,10},{11,12},{13,14},{2,1},{4,3},{6,5},{... | collective-permute-start | bytes 1105928 | tf_op jit(solution)/shard_map/ppermute | solution.py:372
  8.9 21.4 %collective-permute-start = (bf16[2,2,240,384]{3,2,1,0:T(8,128)(2,1)S(1)}, bf16[2,2,240,384]{3,2,1,0:T(8,128)(2,1)S(1)}, u32[]{:S(2)}, u32[]{:S(2)}) collective-permute-start(bf16[2,2,240,384]{3,2,1,0:T(8,128)(2,1)S(1)} %get-tuple-element.26), channel_id=1, source_target_pairs={{0,1},{2,3},{4,5},{6,7},{8,9},{10,11},{12,13},{14,15},{1,0},{3,2},... | collective-permute-start | bytes 2211848 | tf_op jit(solution)/shard_map/ppermute | solution.py:372
  15.9 15.4 %collective-permute-start.2 = (bf16[2,240,384]{2,1,0:T(8,128)(2,1)S(1)}, bf16[2,240,384]{2,1,0:T(8,128)(2,1)S(1)}, u32[]{:S(2)}, u32[]{:S(2)}) collective-permute-start(bf16[2,240,384]{2,1,0:T(8,128)(2,1)S(1)} %get-tuple-element.30), channel_id=1, source_target_pairs={{1,2},{3,4},{5,6},{7,8},{9,10},{11,12},{13,14},{2,1},{4,3},{6,5},{... | collective-permute-start | bytes 1105928 | tf_op jit(solution)/shard_map/ppermute | solution.py:372
  31.8 1.2 %collective-permute-start.3 = (f32[8,128]{1,0:T(8,128)S(1)}, f32[8,128]{1,0:T(8,128)S(1)}, u32[]{:S(2)}, u32[]{:S(2)}) collective-permute-start(f32[8,128]{1,0:T(8,128)S(1)} %get-tuple-element.34.e_ref), channel_id=1, source_target_pairs={{0,16},{16,0},{32,48},{48,32},{64,80},{80,64},{96,112},{112,96},{1... | collective-permute-start | bytes 12296 | tf_op jit(solution)/shard_map/ppermute | solution.py:383
